TPU v7x, 256 devices: a whole 4x4x8 slice. The times are simulated.
256 devices in a mesh: pipe: 16 (over z, core), expert: 16 (over y, x).
Axes of the slice: x: 4, y: 4, z: 8, core: 2. Of those that a mesh axis runs over, the one named last changes fastest.
Arguments:
- tokens: bfloat16 [64, 512, 7168], P('pipe', 'expert'), may hold values from -6 to 6
- up_weight: bfloat16 [16, 7168, 4096], P('pipe', None, 'expert'), may hold values from -0.0625 to 0.0625
- down_weight: bfloat16 [16, 4096, 7168], P('pipe', 'expert'), may hold values from -0.125 to 0.125
- route: int32 [4, 16, 512, 1], P(None, 'pipe', 'expert'), may hold values from 0 to 1; in each aligned block of 32 rows (0 to 31, 32 to 63, ..., all dimensions but the last counted through in order) at most 18 rows name the same one
- gates: float32 [4, 16, 512], P(None, 'pipe', 'expert'), may hold values from 0.3 to 1
Outputs:
- mixed: bfloat16 [64, 512, 7168], P('pipe', 'expert')
Inputs may be any that keep to these rules, and one draw needn't show every extreme that they name: `route`: in every aligned block of 32 tokens along the flattened leading dimensions (one device's tokens of one micro-batch at one step), no expert is named by more than 18 tokens, and some blocks reach 18.
All inputs are finite; a program needn't handle non-finite values.
Results may differ from a plain program's by a relative error of at most 0.0035.
Values may be sent and summed in bfloat16 or wider, within the bound.
No kernel may reach another device: no remote copies, remote signals or barrier semaphores. Data moves between devices by JAX's collectives and lax.ppermute only.
A program may use at most 128 MiB of HBM per device.

v0:
```python
import jax
import jax.numpy as jnp
from jax import lax
from jax.sharding import PartitionSpec as P

D = 7168
EXPERTS = 2
CAP = 18
SIDE = 4
PART = D // SIDE
CUTS = (40, 32)

epsilon = 1e-06


def shift(block, dy, dx):
    pairs = []
    for y in range(SIDE):
        for x in range(SIDE):
            pairs.append((y * SIDE + x, (y + dy) % SIDE * SIDE + (x + dx) % SIDE))
    return lax.ppermute(block, "expert", pairs)


def shift_on(block, dx):
    count = lax.axis_size("pipe")
    pairs = []
    for p in range(count):
        for y in range(SIDE):
            for x in range(SIDE):
                source = p * SIDE * SIDE + y * SIDE + x
                target = (p + 1) % count * SIDE * SIDE + y * SIDE + (x + dx) % SIDE
                pairs.append((source, target))
    return lax.ppermute(block, ("pipe", "expert"), pairs)


def normalize(tok_rows):
    widened = tok_rows.astype(jnp.float32)
    inverse_rms = lax.rsqrt(jnp.mean(widened * widened, axis=-1, keepdims=True) + epsilon)
    return (widened * inverse_rms).astype(jnp.bfloat16)


def slots_of(ids, own):
    rel = (ids != own).astype(jnp.int32)
    count = ids.shape[0]
    member = (rel[:, None] == jnp.arange(EXPERTS, dtype=jnp.int32)[None, :]).astype(jnp.bfloat16)
    earlier = jnp.arange(count)[:, None] > jnp.arange(count)[None, :]
    before = jnp.dot(earlier.astype(jnp.bfloat16), member, preferred_element_type=jnp.float32)
    rank = jnp.sum(before * member.astype(jnp.float32), axis=1).astype(jnp.int32)
    slot, first = 0 * rank, 0
    for size in CUTS:
        inside = (rank >= first) & (rank < first + size)
        slot = jnp.where(inside, EXPERTS * first + rel * size + rank - first, slot)
        first += size
    return slot


def turn(block, step, slots):
    split = block.reshape(SIDE, SIDE, slots, -1)
    return jnp.roll(split, step, axis=1).reshape(block.shape)


def tie(value, *done):
    return lax.optimization_barrier((value, *done))[0]


def exchange(pieces, along_y=False):
    groups = [[y * SIDE + x for x in range(SIDE)] for y in range(SIDE)]
    if along_y:
        groups = [list(group) for group in zip(*groups)]
    return lax.all_to_all(pieces, "expert", 0, 0, axis_index_groups=groups, tiled=True)


def per_device(tokens, up_weight, down_weight, route, gates):
    ticks, _, block, _ = route.shape
    count = ticks * block
    assert sum(CUTS) == ticks * CAP
    place = lax.axis_index("expert")
    y, x = place // SIDE, place % SIDE
    even = y % 2 == 0
    own = y // 2
    up_local, down_local = up_weight[0], down_weight[0]
    depth = up_local.shape[1]
    rows = tokens.reshape(count, D)
    starts = [EXPERTS * sum(CUTS[:c]) for c in range(len(CUTS))]
    cuts = range(len(CUTS))

    def quarter(step):
        return (x + step) % SIDE * PART

    def of(pieces, step):
        return lax.dynamic_index_in_dim(pieces, (x + step) % SIDE, 0, keepdims=False)

    ups = exchange(up_local.reshape(SIDE, PART, depth))
    downs = exchange(jnp.transpose(down_local.reshape(depth, SIDE, PART), (1, 0, 2)))

    slot = slots_of(route.reshape(count), own)
    lanes = jnp.arange(EXPERTS * ticks * CAP, dtype=jnp.int32)
    table = (lanes[:, None] == slot[None, :]).astype(jnp.bfloat16)
    normed = normalize(rows)

    from_x = []
    for step in range(SIDE):
        part = lax.dynamic_slice(normed, (0, quarter(step)), (count, PART))
        message = jnp.dot(table, part, preferred_element_type=jnp.float32).astype(jnp.bfloat16)
        from_x.append(shift(message, 0, step) if step else message)

    received = []
    for c in cuts:
        ours = jnp.stack([r[starts[c] : starts[c] + CUTS[c]] for r in from_x])
        theirs = jnp.stack([r[starts[c] + CUTS[c] : starts[c] + EXPERTS * CUTS[c]] for r in from_x])
        if c:
            ours = tie(ours, ups)
            theirs = tie(theirs, ups)
        sent = [ours, jnp.where(even, ours, theirs), theirs, jnp.where(even, theirs, ours)]
        from_y = [shift(m, step, 0) if step else m for step, m in enumerate(sent)]
        received.append(jnp.stack(from_y).reshape(-1, PART))

    facts = jnp.stack([slot.astype(jnp.float32), gates.reshape(count)])
    rows_before = shift_on(tie(rows, received[0]), 0)
    facts_before = shift_on(tie(facts, received[0]), 0)

    value = 0.0
    for step in range(SIDE):
        partial = []
        for c in cuts:
            product = jnp.dot(received[c], of(ups, -step), preferred_element_type=jnp.float32)
            partial.append(turn(product.astype(jnp.bfloat16), -step, CUTS[c]) if step else product)
        partial = jnp.concatenate(partial)
        if step:
            partial = shift(partial, 0, -step)
        value = value + partial.astype(jnp.float32)
    hidden = jax.nn.silu(tie(value, rows_before, facts_before)).astype(jnp.bfloat16)
    edges = [SIDE * SIDE * sum(CUTS[:c]) for c in range(len(CUTS) + 1)]
    hiddens = [hidden[edges[c] : edges[c + 1]] for c in cuts]

    slot = facts_before[0].astype(jnp.int32)
    table = (slot[:, None] == lanes[None, :]).astype(jnp.bfloat16)
    gathered = []
    for c in cuts:
        sent = tie(hiddens[c], *gathered[0][1:]) if c else hiddens[c]
        gathered.append([shift(turn(sent, step, CUTS[c]), 0, step) if step else sent for step in range(SIDE)])

    combined = [0.0] * SIDE
    landed = []
    for c in cuts:
        out = 0.0
        for step in range(SIDE):
            out = out + jnp.dot(gathered[c][step], of(downs, -step), preferred_element_type=jnp.float32)
        out = out.astype(jnp.bfloat16).reshape(SIDE, SIDE, CUTS[c], PART)
        if c:
            returns = jnp.stack([
                lax.dynamic_index_in_dim(out, (y - target) % SIDE, 0, keepdims=False) for target in range(SIDE)
            ])
            back = tie(exchange(returns, along_y=True), ours, theirs).astype(jnp.float32)
            pairs = [back[0] + back[1], back[2] + back[3]]
            ours = jnp.where(own == 0, pairs[0], pairs[1]).astype(jnp.bfloat16)
            theirs = jnp.where(own == 0, pairs[1], pairs[0]).astype(jnp.bfloat16)
        else:
            back = [(shift(out[step], -step, 0) if step else out[0]).astype(jnp.float32) for step in range(SIDE)]
            ours = (back[0] + jnp.where(even, back[1], back[3])).astype(jnp.bfloat16)
            theirs = (back[2] + jnp.where(even, back[3], back[1])).astype(jnp.bfloat16)
        messages = [jnp.concatenate([ours[step], theirs[step]]) for step in range(SIDE)]
        if c:
            messages = [tie(message, *landed) for message in messages]
        landed = [shift_on(message, -step) for step, message in enumerate(messages)]
        chosen = table[:, starts[c] : starts[c] + EXPERTS * CUTS[c]]
        for step in range(SIDE):
            combined[step] = combined[step] + jnp.dot(chosen, landed[step], preferred_element_type=jnp.float32)

    result = jnp.zeros((count, D), jnp.bfloat16)
    for step in range(SIDE):
        part = lax.dynamic_slice(rows_before, (0, quarter(step)), (count, PART))
        updated = part.astype(jnp.float32) + facts_before[1][:, None] * combined[step]
        result = lax.dynamic_update_slice(result, updated.astype(jnp.bfloat16), (0, quarter(step)))
    return result.reshape(tokens.shape)


def solution(mesh):
    in_specs = (
        P("pipe", "expert", None),
        P("pipe", None, "expert"),
        P("pipe", "expert", None),
        P(None, "pipe", "expert", None),
        P(None, "pipe", "expert"),
    )
    out_specs = P("pipe", "expert", None)
    return jax.shard_map(
        per_device, mesh=mesh, in_specs=in_specs, out_specs=out_specs, check_vma=False
    )
```

profile of v0, /device:TPU:1, one launch (start us, length us, event | category | flops | bytes accessed | tf_op | source)
XLA Modules:
  0.0 259.1 jit_solution(16896718872563172856)
XLA Ops:
  1.1 2.0 multiply_reduce_fusion
  3.2 1.9 multiply_convert_fusion
  6.2 2.0 collective-permute-start
  9.4 2.5 collective-permute-start.1
  14.1 4.9 %all-to-all-start = ((bf16[4,1792,256]{2,1,0:T(8,128)(2,1)}), bf16[4,1792,256]{2,1,0:T(8,128)(2,1)}, u32[]{:S(2)}, u32[]{:S(2)}) async-start(bf16[4,1792,256]{2,1,0:T(8,128)(2,1)} %bitcast.211), calls=%async_computation | async-start | bytes 7340032 | tf_op jit(solution)/shard_map/all_to_all | solution.py:70
  21.6 5.9 %copy.6 = bf16[1,256,7168]{1,2,0:T(8,128)(2,1)} copy(bf16[1,256,7168]{2,1,0:T(8,128)(2,1)} %param.7) | data formatting | bytes 7340032 | tf_op args[2]
  27.5 5.6 %collective-permute-done.1 = bf16[144,1792]{1,0:T(8,128)(2,1)S(1)} collective-permute-done((bf16[144,1792]{1,0:T(8,128)(2,1)}, bf16[144,1792]{1,0:T(8,128)(2,1)S(1)}, u32[]{:S(2)}, u32[]{:S(2)}) %collective-permute-start.1) | collective-permute-done | bytes 516128 | tf_op jit(solution)/shard_map/ppermute | solution.py:21
  34.9 3.2 %collective-permute-start.4 = (bf16[4,40,1792]{2,1,0:T(8,128)(2,1)S(1)}, bf16[4,40,1792]{2,1,0:T(8,128)(2,1)S(1)}, u32[]{:S(2)}, u32[]{:S(2)}) collective-permute-start(bf16[4,40,1792]{2,1,0:T(8,128)(2,1)S(1)} %pad_maximum_fusion.7), channel_id=1, source_target_pairs={{0,8},{1,9},{2,10},{3,11},{4,12},{5,13},{6,14},{7,15},{8,0},{9,1},... | collective-permute-start | bytes 1720328 | tf_op jit(solution)/shard_map/ppermute | solution.py:21
  38.8 2.3 collective-permute-start.5
  42.2 5.3 %collective-permute-done.4 = bf16[4,40,1792]{2,1,0:T(8,128)(2,1)S(1)} collective-permute-done((bf16[4,40,1792]{2,1,0:T(8,128)(2,1)S(1)}, bf16[4,40,1792]{2,1,0:T(8,128)(2,1)S(1)}, u32[]{:S(2)}, u32[]{:S(2)}) %collective-permute-start.4) | collective-permute-done | bytes 573472 | tf_op jit(solution)/shard_map/ppermute | solution.py:21
  47.4 16.5 %collective-permute-done.3 = bf16[4,40,1792]{2,1,0:T(8,128)(2,1)S(1)} collective-permute-done((bf16[4,40,1792]{2,1,0:T(8,128)(2,1)S(1)}, bf16[4,40,1792]{2,1,0:T(8,128)(2,1)S(1)}, u32[]{:S(2)}, u32[]{:S(2)}) %collective-permute-start.3) | collective-permute-done | bytes 573472 | tf_op jit(solution)/shard_map/ppermute | solution.py:21
  65.7 2.3 collective-permute-start.7
  69.6 3.0 %all-to-all-done = bf16[4,1792,256]{2,1,0:T(8,128)(2,1)} async-done(((bf16[4,1792,256]{2,1,0:T(8,128)(2,1)}), bf16[4,1792,256]{2,1,0:T(8,128)(2,1)}, u32[]{:S(2)}, u32[]{:S(2)}) %all-to-all-start) | async-done | bytes 3670048 | tf_op jit(solution)/shard_map/all_to_all | solution.py:70
  72.6 4.8 %all-to-all-start.1 = ((bf16[4,256,1792]{1,2,0:T(8,128)(2,1)}), bf16[4,256,1792]{1,2,0:T(8,128)(2,1)}, u32[]{:S(2)}, u32[]{:S(2)}) async-start(bf16[4,256,1792]{1,2,0:T(8,128)(2,1)} %bitcast.201), calls=%async_computation.1 | async-start | bytes 7340032 | tf_op jit(solution)/shard_map/all_to_all | solution.py:70
  77.4 2.8 %convolution_convert_fusion.6 = bf16[640,256]{1,0:T(8,128)(2,1)S(1)} fusion(bf16[640,1792]{1,0:T(8,128)(2,1)} %bitcast.213, bf16[4,1792,256]{2,1,0:T(8,128)(2,1)} %all-to-all-done, s32[]{:T(128)S(6)} %select_n.266), kind=kOutput, calls=%fused_computation.23 | convolution fusion | flops 587366400 | bytes 3538948 | tf_op jit(solution)/shard_map/dot_general | solution.py:126
  80.3 1.9 convolution_convert_fusion.4
  82.3 3.0 %collective-permute-start.9 = (bf16[4,32,1792]{2,1,0:T(8,128)(2,1)S(1)}, bf16[4,32,1792]{2,1,0:T(8,128)(2,1)S(1)}, u32[]{:S(2)}, u32[]{:S(2)}) collective-permute-start(bf16[4,32,1792]{2,1,0:T(8,128)(2,1)S(1)} %get-tuple-element.19), channel_id=1, source_target_pairs={{0,8},{1,9},{2,10},{3,11},{4,12},{5,13},{6,14},{7,15},{8,0},{9,1},... | collective-permute-start | bytes 1376264 | tf_op jit(solution)/shard_map/ppermute | solution.py:21
  85.8 2.5 collective-permute-start.10
  88.4 1.9 convolution_convert_fusion.5
  90.4 15.8 %collective-permute-done.8 = bf16[4,32,1792]{2,1,0:T(8,128)(2,1)S(1)} collective-permute-done((bf16[4,32,1792]{2,1,0:T(8,128)(2,1)S(1)}, bf16[4,32,1792]{2,1,0:T(8,128)(2,1)S(1)}, u32[]{:S(2)}, u32[]{:S(2)}) %collective-permute-start.8) | collective-permute-done | bytes 458784 | tf_op jit(solution)/shard_map/ppermute | solution.py:21
  106.5 1.8 convolution_convert_fusion.9
  108.4 1.8 convolution_convert_fusion.7
  110.3 2.8 %collective-permute-start.11 = (bf16[1152,256]{1,0:T(8,128)(2,1)S(1)}, bf16[1152,256]{1,0:T(8,128)(2,1)S(1)}, u32[]{:S(2)}, u32[]{:S(2)}) collective-permute-start(bf16[1152,256]{1,0:T(8,128)(2,1)S(1)} %pad_maximum_fusion.3), channel_id=1, source_target_pairs={{0,3},{1,0},{2,1},{3,2},{4,7},{5,4},{6,5},{7,6},{8,11},{9,8},{10,9... | collective-permute-start | bytes 1769480 | tf_op jit(solution)/shard_map/ppermute | solution.py:21
  116.9 1.9 fusion.39
  118.8 1.8 fusion.37
  120.7 13.0 %collective-permute-done.11 = bf16[1152,256]{1,0:T(8,128)(2,1)S(1)} collective-permute-done((bf16[1152,256]{1,0:T(8,128)(2,1)S(1)}, bf16[1152,256]{1,0:T(8,128)(2,1)S(1)}, u32[]{:S(2)}, u32[]{:S(2)}) %collective-permute-start.11) | collective-permute-done | bytes 589856 | tf_op jit(solution)/shard_map/ppermute | solution.py:21
  133.7 12.6 %collective-permute-done.13 = bf16[1152,256]{1,0:T(8,128)(2,1)S(1)} collective-permute-done((bf16[1152,256]{1,0:T(8,128)(2,1)S(1)}, bf16[1152,256]{1,0:T(8,128)(2,1)S(1)}, u32[]{:S(2)}, u32[]{:S(2)}) %collective-permute-start.13) | collective-permute-done | bytes 589856 | tf_op jit(solution)/shard_map/ppermute | solution.py:21
  147.9 2.5 collective-permute-start.16
  150.4 2.0 fusion.29
  152.4 5.1 %collective-permute-done.15 = bf16[640,256]{1,0:T(8,128)(2,1)S(1)} collective-permute-done((bf16[640,256]{1,0:T(8,128)(2,1)S(1)}, bf16[640,256]{1,0:T(8,128)(2,1)S(1)}, u32[]{:S(2)}, u32[]{:S(2)}) %collective-permute-start.15) | collective-permute-done | bytes 327712 | tf_op jit(solution)/shard_map/ppermute | solution.py:21
  157.5 7.8 %collective-permute-done.14 = bf16[640,256]{1,0:T(8,128)(2,1)S(1)} collective-permute-done((bf16[640,256]{1,0:T(8,128)(2,1)S(1)}, bf16[640,256]{1,0:T(8,128)(2,1)S(1)}, u32[]{:S(2)}, u32[]{:S(2)}) %collective-permute-start.14) | collective-permute-done | bytes 327712 | tf_op jit(solution)/shard_map/ppermute | solution.py:21
  165.4 2.0 fusion.21
  167.4 2.0 fusion.25
  169.4 2.1 add_convert_fusion
  172.7 12.5 %collective-permute-start.17 = (bf16[4,40,1792]{2,1,0:T(8,128)(2,1)}, bf16[4,40,1792]{2,1,0:T(8,128)(2,1)}, u32[]{:S(2)}, u32[]{:S(2)}) collective-permute-start(bf16[4,40,1792]{2,1,0:T(8,128)(2,1)} %bitcast.58), channel_id=1, source_target_pairs={{0,12},{1,13},{2,14},{3,15},{4,0},{5,1},{6,2},{7,3},{8,4},{9,5},{1... | collective-permute-start | bytes 1720328 | tf_op jit(solution)/shard_map/ppermute | solution.py:21
  188.5 1.9 fusion.27
  190.4 3.9 %collective-permute-done.21 = bf16[512,256]{1,0:T(8,128)(2,1)S(1)} collective-permute-done((bf16[512,256]{1,0:T(8,128)(2,1)S(1)}, bf16[512,256]{1,0:T(8,128)(2,1)S(1)}, u32[]{:S(2)}, u32[]{:S(2)}) %collective-permute-start.21) | collective-permute-done | bytes 262176 | tf_op jit(solution)/shard_map/ppermute | solution.py:21
  195.4 1.8 fusion.23
  197.2 3.7 %collective-permute-done.22 = bf16[512,256]{1,0:T(8,128)(2,1)S(1)} collective-permute-done((bf16[512,256]{1,0:T(8,128)(2,1)S(1)}, bf16[512,256]{1,0:T(8,128)(2,1)S(1)}, u32[]{:S(2)}, u32[]{:S(2)}) %collective-permute-start.22) | collective-permute-done | bytes 262176 | tf_op jit(solution)/shard_map/ppermute | solution.py:21
  201.0 1.8 fusion.19
  202.8 2.0 add_convert_fusion.1
  206.4 3.6 %all-to-all-start.2 = ((bf16[4,4,32,1792]{3,2,1,0:T(8,128)(2,1)}), bf16[4,4,32,1792]{3,2,1,0:T(8,128)(2,1)S(1)}, u32[]{:S(2)}, u32[]{:S(2)}) async-start(bf16[4,4,32,1792]{3,2,1,0:T(8,128)(2,1)} %pad_maximum_fusion.2), calls=%async_computation.2 | async-start | bytes 3670016 | tf_op jit(solution)/shard_map/all_to_all | solution.py:70
  213.6 3.8 %collective-permute-start.26 = (bf16[80,1792]{1,0:T(8,128)(2,1)S(1)}, bf16[80,1792]{1,0:T(8,128)(2,1)}, u32[]{:S(2)}, u32[]{:S(2)}) collective-permute-start(bf16[80,1792]{1,0:T(8,128)(2,1)S(1)} %pad_maximum_fusion.19), channel_id=1, source_target_pairs={{0,17},{1,18},{2,19},{3,16},{4,21},{5,22},{6,23},{7,20},{8,25},{9,... | collective-permute-start | bytes 860168 | tf_op jit(solution)/shard_map/ppermute | solution.py:33
  218.1 3.8 %collective-permute-start.24 = (bf16[80,1792]{1,0:T(8,128)(2,1)S(1)}, bf16[80,1792]{1,0:T(8,128)(2,1)}, u32[]{:S(2)}, u32[]{:S(2)}) collective-permute-start(bf16[80,1792]{1,0:T(8,128)(2,1)S(1)} %pad_maximum_fusion.17), channel_id=1, source_target_pairs={{0,19},{1,16},{2,17},{3,18},{4,23},{5,20},{6,21},{7,22},{8,27},{9,... | collective-permute-start | bytes 860168 | tf_op jit(solution)/shard_map/ppermute | solution.py:33
  222.4 7.2 %all-to-all-done.2 = bf16[4,4,32,1792]{3,2,1,0:T(8,128)(2,1)S(1)} async-done(((bf16[4,4,32,1792]{3,2,1,0:T(8,128)(2,1)}), bf16[4,4,32,1792]{3,2,1,0:T(8,128)(2,1)S(1)}, u32[]{:S(2)}, u32[]{:S(2)}) %all-to-all-start.2) | async-done | bytes 1835040 | tf_op jit(solution)/shard_map/all_to_all | solution.py:70
  231.4 4.3 %collective-permute-done.24 = bf16[80,1792]{1,0:T(8,128)(2,1)} collective-permute-done((bf16[80,1792]{1,0:T(8,128)(2,1)S(1)}, bf16[80,1792]{1,0:T(8,128)(2,1)}, u32[]{:S(2)}, u32[]{:S(2)}) %collective-permute-start.24) | collective-permute-done | bytes 286752 | tf_op jit(solution)/shard_map/ppermute | solution.py:33
  238.9 3.2 %collective-permute-start.28 = (bf16[64,1792]{1,0:T(8,128)(2,1)S(1)}, bf16[64,1792]{1,0:T(8,128)(2,1)S(1)}, u32[]{:S(2)}, u32[]{:S(2)}) collective-permute-start(bf16[64,1792]{1,0:T(8,128)(2,1)S(1)} %pad_maximum_fusion.27), channel_id=1, source_target_pairs={{0,19},{1,16},{2,17},{3,18},{4,23},{5,20},{6,21},{7,22},{8,27},{9,... | collective-permute-start | bytes 688136 | tf_op jit(solution)/shard_map/ppermute | solution.py:33
  242.2 7.7 %collective-permute-done.30 = bf16[64,1792]{1,0:T(8,128)(2,1)S(1)} collective-permute-done((bf16[64,1792]{1,0:T(8,128)(2,1)S(1)}, bf16[64,1792]{1,0:T(8,128)(2,1)S(1)}, u32[]{:S(2)}, u32[]{:S(2)}) %collective-permute-start.30) | collective-permute-done | bytes 229408 | tf_op jit(solution)/shard_map/ppermute | solution.py:33
  (147 shorter events, 47.3 us)
Async XLA Ops:
  6.2 21.3 %collective-permute-start = (bf16[144,1792]{1,0:T(8,128)(2,1)}, bf16[144,1792]{1,0:T(8,128)(2,1)S(1)}, u32[]{:S(2)}, u32[]{:S(2)}) collective-permute-start(bf16[144,1792]{1,0:T(8,128)(2,1)} %convolution_convert_fusion.2), channel_id=1, source_target_pairs={{0,1},{1,2},{2,3},{3,0},{4,5},{5,6},{6,7},{7,4},{8,9},{9,10},{10,1... | collective-permute-start | bytes 1548296 | tf_op jit(solution)/shard_map/ppermute | solution.py:21
  9.4 23.8 %collective-permute-start.1 = (bf16[144,1792]{1,0:T(8,128)(2,1)}, bf16[144,1792]{1,0:T(8,128)(2,1)S(1)}, u32[]{:S(2)}, u32[]{:S(2)}) collective-permute-start(bf16[144,1792]{1,0:T(8,128)(2,1)} %convolution_convert_fusion.1), channel_id=1, source_target_pairs={{0,2},{1,3},{2,0},{3,1},{4,6},{5,7},{6,4},{7,5},{8,10},{9,11},{10,... | collective-permute-start | bytes 1548296 | tf_op jit(solution)/shard_map/ppermute | solution.py:21
  13.0 20.9 %collective-permute-start.2 = (bf16[144,1792]{1,0:T(8,128)(2,1)}, bf16[144,1792]{1,0:T(8,128)(2,1)}, u32[]{:S(2)}, u32[]{:S(2)}) collective-permute-start(bf16[144,1792]{1,0:T(8,128)(2,1)} %convolution_convert_fusion), channel_id=1, source_target_pairs={{0,3},{1,0},{2,1},{3,2},{4,7},{5,4},{6,5},{7,6},{8,11},{9,8},{10,9... | collective-permute-start | bytes 1548296 | tf_op jit(solution)/shard_map/ppermute | solution.py:21
  14.1 6.0 %copy-start.4 = (f32[4,1,32]{2,1,0:T(1,128)S(1)}, f32[4,1,32]{2,1,0:T(1,128)}, u32[]{:S(2)}) copy-start(f32[4,1,32]{2,1,0:T(1,128)} %param.9) | copy-start | bytes 1540
  14.1 58.5 %all-to-all-start = ((bf16[4,1792,256]{2,1,0:T(8,128)(2,1)}), bf16[4,1792,256]{2,1,0:T(8,128)(2,1)}, u32[]{:S(2)}, u32[]{:S(2)}) async-start(bf16[4,1792,256]{2,1,0:T(8,128)(2,1)} %bitcast.211), calls=%async_computation | async-start | bytes 7340032 | tf_op jit(solution)/shard_map/all_to_all | solution.py:70
  34.9 12.5 %collective-permute-start.4 = (bf16[4,40,1792]{2,1,0:T(8,128)(2,1)S(1)}, bf16[4,40,1792]{2,1,0:T(8,128)(2,1)S(1)}, u32[]{:S(2)}, u32[]{:S(2)}) collective-permute-start(bf16[4,40,1792]{2,1,0:T(8,128)(2,1)S(1)} %pad_maximum_fusion.7), channel_id=1, source_target_pairs={{0,8},{1,9},{2,10},{3,11},{4,12},{5,13},{6,14},{7,15},{8,0},{9,1},... | collective-permute-start | bytes 1720328 | tf_op jit(solution)/shard_map/ppermute | solution.py:21
  38.3 25.7 %collective-permute-start.3 = (bf16[4,40,1792]{2,1,0:T(8,128)(2,1)S(1)}, bf16[4,40,1792]{2,1,0:T(8,128)(2,1)S(1)}, u32[]{:S(2)}, u32[]{:S(2)}) collective-permute-start(bf16[4,40,1792]{2,1,0:T(8,128)(2,1)S(1)} %get-tuple-element.42), channel_id=1, source_target_pairs={{0,4},{1,5},{2,6},{3,7},{4,8},{5,9},{6,10},{7,11},{8,12},{9,13},{1... | collective-permute-start | bytes 1720328 | tf_op jit(solution)/shard_map/ppermute | solution.py:21
  38.8 25.2 %collective-permute-start.5 = (bf16[4,40,1792]{2,1,0:T(8,128)(2,1)S(1)}, bf16[4,40,1792]{2,1,0:T(8,128)(2,1)S(1)}, u32[]{:S(2)}, u32[]{:S(2)}) collective-permute-start(bf16[4,40,1792]{2,1,0:T(8,128)(2,1)S(1)} %get-tuple-element.43), channel_id=1, source_target_pairs={{0,12},{1,13},{2,14},{3,15},{4,0},{5,1},{6,2},{7,3},{8,4},{9,5},{1... | collective-permute-start | bytes 1720328 | tf_op jit(solution)/shard_map/ppermute | solution.py:21
  64.0 4.1 %copy-start.3 = (bf16[1,32,1792]{2,1,0:T(8,128)(2,1)S(1)}, bf16[1,32,1792]{2,1,0:T(8,128)(2,1)}, u32[]{:S(2)}) copy-start(bf16[1,32,1792]{2,1,0:T(8,128)(2,1)} %get-tuple-element.63) | copy-start | bytes 344068
  65.7 2.5 copy-start
  65.7 3.8 %collective-permute-start.7 = (f32[2,128]{1,0:T(2,128)S(1)}, f32[2,128]{1,0:T(2,128)S(1)}, u32[]{:S(2)}, u32[]{:S(2)}) collective-permute-start(f32[2,128]{1,0:T(2,128)S(1)} %pad_maximum_fusion.30), channel_id=1, source_target_pairs={{0,16},{1,17},{2,18},{3,19},{4,20},{5,21},{6,22},{7,23},{8,24},{9,... | collective-permute-start | bytes 3080 | tf_op jit(solution)/shard_map/ppermute | solution.py:33
  68.2 78.4 %collective-permute-start.6 = (bf16[128,7168]{1,0:T(8,128)(2,1)S(1)}, bf16[128,7168]{1,0:T(8,128)(2,1)}, u32[]{:S(2)}, u32[]{:S(2)}) collective-permute-start(bf16[128,7168]{1,0:T(8,128)(2,1)S(1)} %bitcast.205), channel_id=1, source_target_pairs={{0,16},{1,17},{2,18},{3,19},{4,20},{5,21},{6,22},{7,23},{8,24},{9,... | collective-permute-start | bytes 5505032 | tf_op jit(solution)/shard_map/ppermute | solution.py:33
  72.6 77.8 %all-to-all-start.1 = ((bf16[4,256,1792]{1,2,0:T(8,128)(2,1)}), bf16[4,256,1792]{1,2,0:T(8,128)(2,1)}, u32[]{:S(2)}, u32[]{:S(2)}) async-start(bf16[4,256,1792]{1,2,0:T(8,128)(2,1)} %bitcast.201), calls=%async_computation.1 | async-start | bytes 7340032 | tf_op jit(solution)/shard_map/all_to_all | solution.py:70
  77.4 2.8 %copy-start.1 = (bf16[4,4,40,1792]{3,2,1,0:T(8,128)(2,1)S(1)}, bf16[4,4,40,1792]{3,2,1,0:T(8,128)(2,1)}, u32[]{:S(2)}) copy-start(bf16[4,4,40,1792]{3,2,1,0:T(8,128)(2,1)} %pad_maximum_fusion) | copy-start | bytes 6881284
  82.3 24.0 %collective-permute-start.9 = (bf16[4,32,1792]{2,1,0:T(8,128)(2,1)S(1)}, bf16[4,32,1792]{2,1,0:T(8,128)(2,1)S(1)}, u32[]{:S(2)}, u32[]{:S(2)}) collective-permute-start(bf16[4,32,1792]{2,1,0:T(8,128)(2,1)S(1)} %get-tuple-element.19), channel_id=1, source_target_pairs={{0,8},{1,9},{2,10},{3,11},{4,12},{5,13},{6,14},{7,15},{8,0},{9,1},... | collective-permute-start | bytes 1376264 | tf_op jit(solution)/shard_map/ppermute | solution.py:21
  85.3 20.9 %collective-permute-start.8 = (bf16[4,32,1792]{2,1,0:T(8,128)(2,1)S(1)}, bf16[4,32,1792]{2,1,0:T(8,128)(2,1)S(1)}, u32[]{:S(2)}, u32[]{:S(2)}) collective-permute-start(bf16[4,32,1792]{2,1,0:T(8,128)(2,1)S(1)} %get-tuple-element.44), channel_id=1, source_target_pairs={{0,4},{1,5},{2,6},{3,7},{4,8},{5,9},{6,10},{7,11},{8,12},{9,13},{1... | collective-permute-start | bytes 1376264 | tf_op jit(solution)/shard_map/ppermute | solution.py:21
  85.8 20.4 %collective-permute-start.10 = (bf16[4,32,1792]{2,1,0:T(8,128)(2,1)S(1)}, bf16[4,32,1792]{2,1,0:T(8,128)(2,1)S(1)}, u32[]{:S(2)}, u32[]{:S(2)}) collective-permute-start(bf16[4,32,1792]{2,1,0:T(8,128)(2,1)S(1)} %get-tuple-element.45), channel_id=1, source_target_pairs={{0,12},{1,13},{2,14},{3,15},{4,0},{5,1},{6,2},{7,3},{8,4},{9,5},{1... | collective-permute-start | bytes 1376264 | tf_op jit(solution)/shard_map/ppermute | solution.py:21
  110.3 23.4 %collective-permute-start.11 = (bf16[1152,256]{1,0:T(8,128)(2,1)S(1)}, bf16[1152,256]{1,0:T(8,128)(2,1)S(1)}, u32[]{:S(2)}, u32[]{:S(2)}) collective-permute-start(bf16[1152,256]{1,0:T(8,128)(2,1)S(1)} %pad_maximum_fusion.3), channel_id=1, source_target_pairs={{0,3},{1,0},{2,1},{3,2},{4,7},{5,4},{6,5},{7,6},{8,11},{9,8},{10,9... | collective-permute-start | bytes 1769480 | tf_op jit(solution)/shard_map/ppermute | solution.py:21
  115.0 18.7 %collective-permute-start.12 = (bf16[1152,256]{1,0:T(8,128)(2,1)S(1)}, bf16[1152,256]{1,0:T(8,128)(2,1)S(1)}, u32[]{:S(2)}, u32[]{:S(2)}) collective-permute-start(bf16[1152,256]{1,0:T(8,128)(2,1)S(1)} %pad_maximum_fusion.4), channel_id=1, source_target_pairs={{0,2},{1,3},{2,0},{3,1},{4,6},{5,7},{6,4},{7,5},{8,10},{9,11},{10,... | collective-permute-start | bytes 1769480 | tf_op jit(solution)/shard_map/ppermute | solution.py:21
  116.7 29.6 %collective-permute-start.13 = (bf16[1152,256]{1,0:T(8,128)(2,1)S(1)}, bf16[1152,256]{1,0:T(8,128)(2,1)S(1)}, u32[]{:S(2)}, u32[]{:S(2)}) collective-permute-start(bf16[1152,256]{1,0:T(8,128)(2,1)S(1)} %pad_maximum_fusion.5), channel_id=1, source_target_pairs={{0,1},{1,2},{2,3},{3,0},{4,5},{5,6},{6,7},{7,4},{8,9},{9,10},{10,1... | collective-permute-start | bytes 1769480 | tf_op jit(solution)/shard_map/ppermute | solution.py:21
  147.0 10.4 %collective-permute-start.15 = (bf16[640,256]{1,0:T(8,128)(2,1)S(1)}, bf16[640,256]{1,0:T(8,128)(2,1)S(1)}, u32[]{:S(2)}, u32[]{:S(2)}) collective-permute-start(bf16[640,256]{1,0:T(8,128)(2,1)S(1)} %bitcast.234), channel_id=1, source_target_pairs={{0,2},{1,3},{2,0},{3,1},{4,6},{5,7},{6,4},{7,5},{8,10},{9,11},{10,... | collective-permute-start | bytes 983048 | tf_op jit(solution)/shard_map/ppermute | solution.py:21
  147.5 17.8 %collective-permute-start.14 = (bf16[640,256]{1,0:T(8,128)(2,1)S(1)}, bf16[640,256]{1,0:T(8,128)(2,1)S(1)}, u32[]{:S(2)}, u32[]{:S(2)}) collective-permute-start(bf16[640,256]{1,0:T(8,128)(2,1)S(1)} %bitcast.235), channel_id=1, source_target_pairs={{0,1},{1,2},{2,3},{3,0},{4,5},{5,6},{6,7},{7,4},{8,9},{9,10},{10,1... | collective-permute-start | bytes 983048 | tf_op jit(solution)/shard_map/ppermute | solution.py:21
  147.9 17.4 %collective-permute-start.16 = (bf16[640,256]{1,0:T(8,128)(2,1)S(1)}, bf16[640,256]{1,0:T(8,128)(2,1)S(1)}, u32[]{:S(2)}, u32[]{:S(2)}) collective-permute-start(bf16[640,256]{1,0:T(8,128)(2,1)S(1)} %bitcast.236), channel_id=1, source_target_pairs={{0,3},{1,0},{2,1},{3,2},{4,7},{5,4},{6,5},{7,6},{8,11},{9,8},{10,9... | collective-permute-start | bytes 983048 | tf_op jit(solution)/shard_map/ppermute | solution.py:21
  172.7 37.3 %collective-permute-start.17 = (bf16[4,40,1792]{2,1,0:T(8,128)(2,1)}, bf16[4,40,1792]{2,1,0:T(8,128)(2,1)}, u32[]{:S(2)}, u32[]{:S(2)}) collective-permute-start(bf16[4,40,1792]{2,1,0:T(8,128)(2,1)} %bitcast.58), channel_id=1, source_target_pairs={{0,12},{1,13},{2,14},{3,15},{4,0},{5,1},{6,2},{7,3},{8,4},{9,5},{1... | collective-permute-start | bytes 1720328 | tf_op jit(solution)/shard_map/ppermute | solution.py:21
  185.2 24.9 %collective-permute-start.18 = (bf16[4,40,1792]{2,1,0:T(8,128)(2,1)}, bf16[4,40,1792]{2,1,0:T(8,128)(2,1)}, u32[]{:S(2)}, u32[]{:S(2)}) collective-permute-start(bf16[4,40,1792]{2,1,0:T(8,128)(2,1)} %bitcast.59), channel_id=1, source_target_pairs={{0,4},{1,5},{2,6},{3,7},{4,8},{5,9},{6,10},{7,11},{8,12},{9,13},{1... | collective-permute-start | bytes 1720328 | tf_op jit(solution)/shard_map/ppermute | solution.py:21
  185.2 26.5 %collective-permute-start.19 = (bf16[4,40,1792]{2,1,0:T(8,128)(2,1)S(1)}, bf16[4,40,1792]{2,1,0:T(8,128)(2,1)}, u32[]{:S(2)}, u32[]{:S(2)}) collective-permute-start(bf16[4,40,1792]{2,1,0:T(8,128)(2,1)S(1)} %bitcast.227), channel_id=1, source_target_pairs={{0,8},{1,9},{2,10},{3,11},{4,12},{5,13},{6,14},{7,15},{8,0},{9,1},... | collective-permute-start | bytes 1720328 | tf_op jit(solution)/shard_map/ppermute | solution.py:21
  186.8 16.0 %collective-permute-start.23 = (bf16[512,256]{1,0:T(8,128)(2,1)S(1)}, bf16[512,256]{1,0:T(8,128)(2,1)S(1)}, u32[]{:S(2)}, u32[]{:S(2)}) collective-permute-start(bf16[512,256]{1,0:T(8,128)(2,1)S(1)} %bitcast.246), channel_id=1, source_target_pairs={{0,3},{1,0},{2,1},{3,2},{4,7},{5,4},{6,5},{7,6},{8,11},{9,8},{10,9... | collective-permute-start | bytes 786440 | tf_op jit(solution)/shard_map/ppermute | solution.py:21
  187.0 7.3 %collective-permute-start.21 = (bf16[512,256]{1,0:T(8,128)(2,1)S(1)}, bf16[512,256]{1,0:T(8,128)(2,1)S(1)}, u32[]{:S(2)}, u32[]{:S(2)}) collective-permute-start(bf16[512,256]{1,0:T(8,128)(2,1)S(1)} %bitcast.248), channel_id=1, source_target_pairs={{0,1},{1,2},{2,3},{3,0},{4,5},{5,6},{6,7},{7,4},{8,9},{9,10},{10,1... | collective-permute-start | bytes 786440 | tf_op jit(solution)/shard_map/ppermute | solution.py:21
  194.2 6.7 %collective-permute-start.22 = (bf16[512,256]{1,0:T(8,128)(2,1)S(1)}, bf16[512,256]{1,0:T(8,128)(2,1)S(1)}, u32[]{:S(2)}, u32[]{:S(2)}) collective-permute-start(bf16[512,256]{1,0:T(8,128)(2,1)S(1)} %bitcast.247), channel_id=1, source_target_pairs={{0,2},{1,3},{2,0},{3,1},{4,6},{5,7},{6,4},{7,5},{8,10},{9,11},{10,... | collective-permute-start | bytes 786440 | tf_op jit(solution)/shard_map/ppermute | solution.py:21
  206.4 23.2 %all-to-all-start.2 = ((bf16[4,4,32,1792]{3,2,1,0:T(8,128)(2,1)}), bf16[4,4,32,1792]{3,2,1,0:T(8,128)(2,1)S(1)}, u32[]{:S(2)}, u32[]{:S(2)}) async-start(bf16[4,4,32,1792]{3,2,1,0:T(8,128)(2,1)} %pad_maximum_fusion.2), calls=%async_computation.2 | async-start | bytes 3670016 | tf_op jit(solution)/shard_map/all_to_all | solution.py:70
  213.6 16.8 %collective-permute-start.26 = (bf16[80,1792]{1,0:T(8,128)(2,1)S(1)}, bf16[80,1792]{1,0:T(8,128)(2,1)}, u32[]{:S(2)}, u32[]{:S(2)}) collective-permute-start(bf16[80,1792]{1,0:T(8,128)(2,1)S(1)} %pad_maximum_fusion.19), channel_id=1, source_target_pairs={{0,17},{1,18},{2,19},{3,16},{4,21},{5,22},{6,23},{7,20},{8,25},{9,... | collective-permute-start | bytes 860168 | tf_op jit(solution)/shard_map/ppermute | solution.py:33
  217.4 14.0 %collective-permute-start.25 = (bf16[80,1792]{1,0:T(8,128)(2,1)S(1)}, bf16[80,1792]{1,0:T(8,128)(2,1)}, u32[]{:S(2)}, u32[]{:S(2)}) collective-permute-start(bf16[80,1792]{1,0:T(8,128)(2,1)S(1)} %pad_maximum_fusion.18), channel_id=1, source_target_pairs={{0,18},{1,19},{2,16},{3,17},{4,22},{5,23},{6,20},{7,21},{8,26},{9,... | collective-permute-start | bytes 860168 | tf_op jit(solution)/shard_map/ppermute | solution.py:33
  218.1 17.6 %collective-permute-start.24 = (bf16[80,1792]{1,0:T(8,128)(2,1)S(1)}, bf16[80,1792]{1,0:T(8,128)(2,1)}, u32[]{:S(2)}, u32[]{:S(2)}) collective-permute-start(bf16[80,1792]{1,0:T(8,128)(2,1)S(1)} %pad_maximum_fusion.17), channel_id=1, source_target_pairs={{0,19},{1,16},{2,17},{3,18},{4,23},{5,20},{6,21},{7,22},{8,27},{9,... | collective-permute-start | bytes 860168 | tf_op jit(solution)/shard_map/ppermute | solution.py:33
  221.9 13.8 %collective-permute-start.20 = (bf16[80,1792]{1,0:T(8,128)(2,1)S(1)}, bf16[80,1792]{1,0:T(8,128)(2,1)S(1)}, u32[]{:S(2)}, u32[]{:S(2)}) collective-permute-start(bf16[80,1792]{1,0:T(8,128)(2,1)S(1)} %pad_maximum_fusion.16), channel_id=1, source_target_pairs={{0,16},{1,17},{2,18},{3,19},{4,20},{5,21},{6,22},{7,23},{8,24},{9,... | collective-permute-start | bytes 860168 | tf_op jit(solution)/shard_map/ppermute | solution.py:33
  235.7 14.3 %collective-permute-start.30 = (bf16[64,1792]{1,0:T(8,128)(2,1)S(1)}, bf16[64,1792]{1,0:T(8,128)(2,1)S(1)}, u32[]{:S(2)}, u32[]{:S(2)}) collective-permute-start(bf16[64,1792]{1,0:T(8,128)(2,1)S(1)} %pad_maximum_fusion.29), channel_id=1, source_target_pairs={{0,17},{1,18},{2,19},{3,16},{4,21},{5,22},{6,23},{7,20},{8,25},{9,... | collective-permute-start | bytes 688136 | tf_op jit(solution)/shard_map/ppermute | solution.py:33
  237.5 12.8 %collective-permute-start.29 = (bf16[64,1792]{1,0:T(8,128)(2,1)S(1)}, bf16[64,1792]{1,0:T(8,128)(2,1)S(1)}, u32[]{:S(2)}, u32[]{:S(2)}) collective-permute-start(bf16[64,1792]{1,0:T(8,128)(2,1)S(1)} %pad_maximum_fusion.28), channel_id=1, source_target_pairs={{0,18},{1,19},{2,16},{3,17},{4,22},{5,23},{6,20},{7,21},{8,26},{9,... | collective-permute-start | bytes 688136 | tf_op jit(solution)/shard_map/ppermute | solution.py:33
  238.9 12.4 %collective-permute-start.28 = (bf16[64,1792]{1,0:T(8,128)(2,1)S(1)}, bf16[64,1792]{1,0:T(8,128)(2,1)S(1)}, u32[]{:S(2)}, u32[]{:S(2)}) collective-permute-start(bf16[64,1792]{1,0:T(8,128)(2,1)S(1)} %pad_maximum_fusion.27), channel_id=1, source_target_pairs={{0,19},{1,16},{2,17},{3,18},{4,23},{5,20},{6,21},{7,22},{8,27},{9,... | collective-permute-start | bytes 688136 | tf_op jit(solution)/shard_map/ppermute | solution.py:33
  242.2 9.4 %collective-permute-start.27 = (bf16[64,1792]{1,0:T(8,128)(2,1)S(1)}, bf16[64,1792]{1,0:T(8,128)(2,1)S(1)}, u32[]{:S(2)}, u32[]{:S(2)}) collective-permute-start(bf16[64,1792]{1,0:T(8,128)(2,1)S(1)} %pad_maximum_fusion.26), channel_id=1, source_target_pairs={{0,16},{1,17},{2,18},{3,19},{4,20},{5,21},{6,22},{7,23},{8,24},{9,... | collective-permute-start | bytes 688136 | tf_op jit(solution)/shard_map/ppermute | solution.py:33
  257.7 1.2 copy-start.2
where the time goes:
time: 264 us; the launch traced here: 259 us
  waiting for transfers between devices  116 us (44%)
  starting transfers between devices  74.4 us (28%)
  matrix products  42.2 us (16%)
  local copies, waits for them, and re-layouts  13 us (5%)
  other arithmetic  12.9 us (5%)
    ppermute x21, waiting for transfers between devices, shift(): return lax.ppermute(block, 'expert', pairs)  91.7 us
    ppermute x21, starting transfers between devices, shift(): return lax.ppermute(block, 'expert', pairs)  42.1 us
    ppermute x10, starting transfers between devices, shift_on(): return lax.ppermute(block, ('pipe', 'expert'), pairs)  19 us
    dot_general x8, matrix products, per_device(): jnp.dot(received[c], of(ups, -step), preferred_element_type=jnp.float32)  15.9 us
    dot_general x8, matrix products, per_device(): jnp.dot(gathered[c][step], of(downs, -step), preferred_element_type=jnp.f...  15.6 us
    ppermute x10, waiting for transfers between devices, shift_on(): return lax.ppermute(block, ('pipe', 'expert'), pairs)  13.7 us
    all_to_all x3, starting transfers between devices, exchange(): lax.all_to_all(pieces, 'expert', 0, 0, axis_index_groups=groups, tiled=True)  13.3 us
    all_to_all x3, waiting for transfers between devices, exchange(): lax.all_to_all(pieces, 'expert', 0, 0, axis_index_groups=groups, tiled=True)  10.3 us
  transfers between devices with their start and end apart: 34, of which 18 were waited for; matrix products, arithmetic and copies ran while one was open for 18% of the time, Pallas kernels for 0%

commit v1 on v0

--- a/solution.py
+++ b/solution.py
@@ -137,15 +137,16 @@
     table = (slot[:, None] == lanes[None, :]).astype(jnp.bfloat16)
     gathered = []
     for c in cuts:
-        sent = tie(hiddens[c], *gathered[0][1:]) if c else hiddens[c]
+        sent = tie(hiddens[c], gathered[0][2]) if c else hiddens[c]
         gathered.append([shift(turn(sent, step, CUTS[c]), 0, step) if step else sent for step in range(SIDE)])
+
+    downs = tie(downs, hidden)
+    down = jnp.concatenate([of(downs, -step) for step in range(SIDE)])
 
     combined = [0.0] * SIDE
     landed = []
     for c in cuts:
-        out = 0.0
-        for step in range(SIDE):
-            out = out + jnp.dot(gathered[c][step], of(downs, -step), preferred_element_type=jnp.float32)
+        out = jnp.dot(jnp.concatenate(gathered[c], axis=1), down, preferred_element_type=jnp.float32)
         out = out.astype(jnp.bfloat16).reshape(SIDE, SIDE, CUTS[c], PART)
         if c:
             returns = jnp.stack([

time: 264 us -> 267 us (1.011)
  matrix products: 42.2 us -> 32.4 us
  starting transfers between devices: 74.4 us -> 82.5 us
  local copies, waits for them, and re-layouts: 13 us -> 21 us
  waiting for transfers between devices: 116 us -> 111 us
  other arithmetic: 12.9 us -> 15.8 us
    dot_general x8 -> x2, matrix products: 15.6 us -> 5.78 us  [per_device(): jnp.dot(jnp.concatenate(gathered[c], axis=1), down, preferred_element_typ...]
    dynamic_slice x0 -> x5, local copies, waits for them, and re-layouts: none -> 7.99 us  [of(): lax.dynamic_index_in_dim(pieces, (x + step) % SIDE, 0, keepdims=False)]
    ppermute x10, starting transfers between devices: 19 us -> 25.9 us  [shift_on(): return lax.ppermute(block, ('pipe', 'expert'), pairs)]
    all_to_all x3, waiting for transfers between devices: 10.3 us -> 4.05 us  [exchange(): lax.all_to_all(pieces, 'expert', 0, 0, axis_index_groups=groups, tiled=True)]
    ppermute x10, waiting for transfers between devices: 13.7 us -> 18.6 us  [shift_on(): return lax.ppermute(block, ('pipe', 'expert'), pairs)]
    ppermute x21, waiting for transfers between devices: 91.7 us -> 88.3 us  [shift(): return lax.ppermute(block, 'expert', pairs)]
    unnamed x12 -> x20, local copies, waits for them, and re-layouts: 7.74 us -> 7.71 us
  transfers between devices with their start and end apart: 34 -> 34, of which waited for: 18 -> 16; matrix products, arithmetic and copies ran while one was open for 18% -> 21% of each run, Pallas kernels for 0% -> 0%
where the time goes in v1:
time: 267 us; the launch traced here: 264 us
  waiting for transfers between devices  111 us (42%)
  starting transfers between devices  82.5 us (31%)
  matrix products  32.4 us (12%)
  local copies, waits for them, and re-layouts  21 us (8%)
  other arithmetic  15.8 us (6%)
    ppermute x21, waiting for transfers between devices, shift(): return lax.ppermute(block, 'expert', pairs)  88.3 us
    ppermute x21, starting transfers between devices, shift(): return lax.ppermute(block, 'expert', pairs)  43.4 us
    ppermute x10, starting transfers between devices, shift_on(): return lax.ppermute(block, ('pipe', 'expert'), pairs)  25.9 us
    ppermute x10, waiting for transfers between devices, shift_on(): return lax.ppermute(block, ('pipe', 'expert'), pairs)  18.6 us
    dot_general x8, matrix products, per_device(): jnp.dot(received[c], of(ups, -step), preferred_element_type=jnp.float32)  15.9 us
    all_to_all x3, starting transfers between devices, exchange(): lax.all_to_all(pieces, 'expert', 0, 0, axis_index_groups=groups, tiled=True)  13.3 us
    dynamic_slice x5, local copies, waits for them, and re-layouts, of(): lax.dynamic_index_in_dim(pieces, (x + step) % SIDE, 0, keepdims=False)  7.99 us
    unnamed x20, local copies, waits for them, and re-layouts  7.71 us
  transfers between devices with their start and end apart: 34, of which 16 were waited for; matrix products, arithmetic and copies ran while one was open for 21% of the time, Pallas kernels for 0%

profile of v1, /device:TPU:1, one launch (start us, length us, event | category | flops | bytes accessed | tf_op | source)
XLA Modules:
  0.0 263.7 jit_solution(4346151894307800220)
XLA Ops:
  1.1 2.0 multiply_reduce_fusion
  3.2 1.9 multiply_convert_fusion
  6.2 2.0 collective-permute-start
  9.4 2.5 collective-permute-start.1
  14.1 4.9 %all-to-all-start = ((bf16[4,1792,256]{2,1,0:T(8,128)(2,1)}), bf16[4,1792,256]{2,1,0:T(8,128)(2,1)}, u32[]{:S(2)}, u32[]{:S(2)}) async-start(bf16[4,1792,256]{2,1,0:T(8,128)(2,1)} %bitcast.175), calls=%async_computation | async-start | bytes 7340032 | tf_op jit(solution)/shard_map/all_to_all | solution.py:70
  21.5 5.9 %copy.6 = bf16[1,256,7168]{1,2,0:T(8,128)(2,1)} copy(bf16[1,256,7168]{2,1,0:T(8,128)(2,1)} %param.7) | data formatting | bytes 7340032 | tf_op args[2]
  27.4 5.8 %collective-permute-done.1 = bf16[144,1792]{1,0:T(8,128)(2,1)S(1)} collective-permute-done((bf16[144,1792]{1,0:T(8,128)(2,1)}, bf16[144,1792]{1,0:T(8,128)(2,1)S(1)}, u32[]{:S(2)}, u32[]{:S(2)}) %collective-permute-start.1) | collective-permute-done | bytes 516128 | tf_op jit(solution)/shard_map/ppermute | solution.py:21
  34.9 3.2 %collective-permute-start.4 = (bf16[4,40,1792]{2,1,0:T(8,128)(2,1)S(1)}, bf16[4,40,1792]{2,1,0:T(8,128)(2,1)S(1)}, u32[]{:S(2)}, u32[]{:S(2)}) collective-permute-start(bf16[4,40,1792]{2,1,0:T(8,128)(2,1)S(1)} %pad_maximum_fusion.10), channel_id=1, source_target_pairs={{0,8},{1,9},{2,10},{3,11},{4,12},{5,13},{6,14},{7,15},{8,0},{9,1},... | collective-permute-start | bytes 1720328 | tf_op jit(solution)/shard_map/ppermute | solution.py:21
  38.8 2.3 collective-permute-start.5
  42.2 5.3 %collective-permute-done.4 = bf16[4,40,1792]{2,1,0:T(8,128)(2,1)S(1)} collective-permute-done((bf16[4,40,1792]{2,1,0:T(8,128)(2,1)S(1)}, bf16[4,40,1792]{2,1,0:T(8,128)(2,1)S(1)}, u32[]{:S(2)}, u32[]{:S(2)}) %collective-permute-start.4) | collective-permute-done | bytes 573472 | tf_op jit(solution)/shard_map/ppermute | solution.py:21
  47.4 16.5 %collective-permute-done.3 = bf16[4,40,1792]{2,1,0:T(8,128)(2,1)S(1)} collective-permute-done((bf16[4,40,1792]{2,1,0:T(8,128)(2,1)S(1)}, bf16[4,40,1792]{2,1,0:T(8,128)(2,1)S(1)}, u32[]{:S(2)}, u32[]{:S(2)}) %collective-permute-start.3) | collective-permute-done | bytes 573472 | tf_op jit(solution)/shard_map/ppermute | solution.py:21
  64.0 1.8 pad_maximum_fusion.1
  65.7 2.3 collective-permute-start.7
  69.6 3.1 %all-to-all-done = bf16[4,1792,256]{2,1,0:T(8,128)(2,1)} async-done(((bf16[4,1792,256]{2,1,0:T(8,128)(2,1)}), bf16[4,1792,256]{2,1,0:T(8,128)(2,1)}, u32[]{:S(2)}, u32[]{:S(2)}) %all-to-all-start) | async-done | bytes 3670048 | tf_op jit(solution)/shard_map/all_to_all | solution.py:70
  72.6 4.8 %all-to-all-start.1 = ((bf16[4,256,1792]{1,2,0:T(8,128)(2,1)}), bf16[4,256,1792]{1,2,0:T(8,128)(2,1)}, u32[]{:S(2)}, u32[]{:S(2)}) async-start(bf16[4,256,1792]{1,2,0:T(8,128)(2,1)} %bitcast.166), calls=%async_computation.1 | async-start | bytes 7340032 | tf_op jit(solution)/shard_map/all_to_all | solution.py:70
  77.4 2.8 %convolution_convert_fusion.8 = bf16[640,256]{1,0:T(8,128)(2,1)S(1)} fusion(bf16[640,1792]{1,0:T(8,128)(2,1)} %bitcast.177, bf16[4,1792,256]{2,1,0:T(8,128)(2,1)} %all-to-all-done, s32[]{:T(128)S(6)} %select_n.254), kind=kOutput, calls=%fused_computation.31 | convolution fusion | flops 587366400 | bytes 3538948 | tf_op jit(solution)/shard_map/dot_general | solution.py:126
  80.3 1.9 convolution_convert_fusion.6
  82.3 3.0 %collective-permute-start.9 = (bf16[4,32,1792]{2,1,0:T(8,128)(2,1)S(1)}, bf16[4,32,1792]{2,1,0:T(8,128)(2,1)S(1)}, u32[]{:S(2)}, u32[]{:S(2)}) collective-permute-start(bf16[4,32,1792]{2,1,0:T(8,128)(2,1)S(1)} %get-tuple-element.20), channel_id=1, source_target_pairs={{0,8},{1,9},{2,10},{3,11},{4,12},{5,13},{6,14},{7,15},{8,0},{9,1},... | collective-permute-start | bytes 1376264 | tf_op jit(solution)/shard_map/ppermute | solution.py:21
  85.8 2.5 collective-permute-start.10
  88.4 1.9 convolution_convert_fusion.7
  90.4 15.8 %collective-permute-done.8 = bf16[4,32,1792]{2,1,0:T(8,128)(2,1)S(1)} collective-permute-done((bf16[4,32,1792]{2,1,0:T(8,128)(2,1)S(1)}, bf16[4,32,1792]{2,1,0:T(8,128)(2,1)S(1)}, u32[]{:S(2)}, u32[]{:S(2)}) %collective-permute-start.8) | collective-permute-done | bytes 458784 | tf_op jit(solution)/shard_map/ppermute | solution.py:21
  106.5 1.8 convolution_convert_fusion.11
  108.3 1.8 convolution_convert_fusion.9
  110.3 2.8 %collective-permute-start.11 = (bf16[1152,256]{1,0:T(8,128)(2,1)S(1)}, bf16[1152,256]{1,0:T(8,128)(2,1)S(1)}, u32[]{:S(2)}, u32[]{:S(2)}) collective-permute-start(bf16[1152,256]{1,0:T(8,128)(2,1)S(1)} %pad_maximum_fusion.6), channel_id=1, source_target_pairs={{0,3},{1,0},{2,1},{3,2},{4,7},{5,4},{6,5},{7,6},{8,11},{9,8},{10,9... | collective-permute-start | bytes 1769480 | tf_op jit(solution)/shard_map/ppermute | solution.py:21
  113.1 1.8 convolution_convert_fusion.10
  116.9 1.9 fusion.33
  118.8 1.8 fusion.31
  120.6 13.0 %collective-permute-done.11 = bf16[1152,256]{1,0:T(8,128)(2,1)S(1)} collective-permute-done((bf16[1152,256]{1,0:T(8,128)(2,1)S(1)}, bf16[1152,256]{1,0:T(8,128)(2,1)S(1)}, u32[]{:S(2)}, u32[]{:S(2)}) %collective-permute-start.11) | collective-permute-done | bytes 589856 | tf_op jit(solution)/shard_map/ppermute | solution.py:21
  133.7 12.6 %collective-permute-done.13 = bf16[1152,256]{1,0:T(8,128)(2,1)S(1)} collective-permute-done((bf16[1152,256]{1,0:T(8,128)(2,1)S(1)}, bf16[1152,256]{1,0:T(8,128)(2,1)S(1)}, u32[]{:S(2)}, u32[]{:S(2)}) %collective-permute-start.13) | collective-permute-done | bytes 589856 | tf_op jit(solution)/shard_map/ppermute | solution.py:21
  148.6 2.7 %collective-permute-start.16 = (bf16[640,256]{1,0:T(8,128)(2,1)}, bf16[640,256]{1,0:T(8,128)(2,1)}, u32[]{:S(2)}, u32[]{:S(2)}) collective-permute-start(bf16[640,256]{1,0:T(8,128)(2,1)} %bitcast.50), channel_id=1, source_target_pairs={{0,3},{1,0},{2,1},{3,2},{4,7},{5,4},{6,5},{7,6},{8,11},{9,8},{10,9... | collective-permute-start | bytes 983048 | tf_op jit(solution)/shard_map/ppermute | solution.py:21
  152.1 3.2 %constant_dynamic-slice_fusion.7 = (bf16[1,256,1792]{1,2,0:T(8,128)(2,1)}, bf16[1,256,1792]{1,2,0:T(8,128)(2,1)S(1)}, bf16[1,256,1792]{1,2,0:T(8,128)(2,1)S(1)}, bf16[1,256,1792]{1,2,0:T(8,128)(2,1)S(1)}) fusion(bf16[4,256,1792]{1,2,0:T(8,128)(2,1)} %all-to-all-done.1, s32[]{:T(128)S(6)} %select_n.249, s32[]{:T(128)S(6)} %select_n.258, s32[]{:T(128)S(6)} %select_n.256, ...), kind=kLoop, calls=%fused_computation.178 | loop fusion | bytes 7340048 | tf_op jit(solution)/shard_map/jit(dynamic_index_in_dim)/dynamic_slice | solution.py:91
  155.2 2.2 copy.7
  160.1 3.6 %collective-permute-done.15 = bf16[640,256]{1,0:T(8,128)(2,1)} collective-permute-done((bf16[640,256]{1,0:T(8,128)(2,1)}, bf16[640,256]{1,0:T(8,128)(2,1)}, u32[]{:S(2)}, u32[]{:S(2)}) %collective-permute-start.15) | collective-permute-done | bytes 327712 | tf_op jit(solution)/shard_map/ppermute | solution.py:21
  165.6 2.4 collective-permute-start.22
  168.0 10.2 %collective-permute-start.23 = (bf16[512,256]{1,0:T(8,128)(2,1)S(1)}, bf16[512,256]{1,0:T(8,128)(2,1)S(1)}, u32[]{:S(2)}, u32[]{:S(2)}) collective-permute-start(bf16[512,256]{1,0:T(8,128)(2,1)S(1)} %bitcast.217), channel_id=1, source_target_pairs={{0,3},{1,0},{2,1},{3,2},{4,7},{5,4},{6,5},{7,6},{8,11},{9,8},{10,9... | collective-permute-start | bytes 786440 | tf_op jit(solution)/shard_map/ppermute | solution.py:21
  178.2 3.7 %convolution_convert_fusion = bf16[640,1792]{1,0:T(8,128)(2,1)S(1)} fusion(bf16[640,256]{1,0:T(8,128)(2,1)} %collective-permute-done.16, bf16[640,256]{1,0:T(8,128)(2,1)} %collective-permute-done.15, bf16[640,256]{1,0:T(8,128)(2,1)} %collective-permute-done.14, bf16[640,256]{1,0:T(8,128)(2,1)S(1)} %slice.348, bf16[256,1792]{1,0:T(8,128)(2,1)S(1)} %bitcast.198, ...), kind=kOutput, calls=%fused_computation.3 | convolution fusion | flops 2369880064 | bytes 7274496 | tf_op jit(solution)/shard_map/dot_general | solution.py:149
  183.2 2.7 %collective-permute-start.17 = (bf16[4,40,1792]{2,1,0:T(8,128)(2,1)}, bf16[4,40,1792]{2,1,0:T(8,128)(2,1)}, u32[]{:S(2)}, u32[]{:S(2)}) collective-permute-start(bf16[4,40,1792]{2,1,0:T(8,128)(2,1)} %bitcast.58), channel_id=1, source_target_pairs={{0,12},{1,13},{2,14},{3,15},{4,0},{5,1},{6,2},{7,3},{8,4},{9,5},{1... | collective-permute-start | bytes 1720328 | tf_op jit(solution)/shard_map/ppermute | solution.py:21
  187.6 2.1 convolution_convert_fusion.1
  191.3 3.6 %all-to-all-start.2 = ((bf16[4,4,32,1792]{3,2,1,0:T(8,128)(2,1)}), bf16[4,4,32,1792]{3,2,1,0:T(8,128)(2,1)S(1)}, u32[]{:S(2)}, u32[]{:S(2)}) async-start(bf16[4,4,32,1792]{3,2,1,0:T(8,128)(2,1)} %pad_maximum_fusion.3), calls=%async_computation.2 | async-start | bytes 3670016 | tf_op jit(solution)/shard_map/all_to_all | solution.py:70
  196.6 3.1 %collective-permute-done.18 = bf16[4,40,1792]{2,1,0:T(8,128)(2,1)} collective-permute-done((bf16[4,40,1792]{2,1,0:T(8,128)(2,1)}, bf16[4,40,1792]{2,1,0:T(8,128)(2,1)}, u32[]{:S(2)}, u32[]{:S(2)}) %collective-permute-start.18) | collective-permute-done | bytes 573472 | tf_op jit(solution)/shard_map/ppermute | solution.py:21
  199.7 10.3 %collective-permute-done.19 = bf16[4,40,1792]{2,1,0:T(8,128)(2,1)} collective-permute-done((bf16[4,40,1792]{2,1,0:T(8,128)(2,1)}, bf16[4,40,1792]{2,1,0:T(8,128)(2,1)}, u32[]{:S(2)}, u32[]{:S(2)}) %collective-permute-start.19) | collective-permute-done | bytes 573472 | tf_op jit(solution)/shard_map/ppermute | solution.py:21
  211.8 11.6 %collective-permute-start.26 = (bf16[80,1792]{1,0:T(8,128)(2,1)S(1)}, bf16[80,1792]{1,0:T(8,128)(2,1)}, u32[]{:S(2)}, u32[]{:S(2)}) collective-permute-start(bf16[80,1792]{1,0:T(8,128)(2,1)S(1)} %pad_maximum_fusion.22), channel_id=1, source_target_pairs={{0,17},{1,18},{2,19},{3,16},{4,21},{5,22},{6,23},{7,20},{8,25},{9,... | collective-permute-start | bytes 860168 | tf_op jit(solution)/shard_map/ppermute | solution.py:33
  224.2 3.2 %collective-permute-start.24 = (bf16[80,1792]{1,0:T(8,128)(2,1)S(1)}, bf16[80,1792]{1,0:T(8,128)(2,1)}, u32[]{:S(2)}, u32[]{:S(2)}) collective-permute-start(bf16[80,1792]{1,0:T(8,128)(2,1)S(1)} %pad_maximum_fusion.20), channel_id=1, source_target_pairs={{0,19},{1,16},{2,17},{3,18},{4,23},{5,20},{6,21},{7,22},{8,27},{9,... | collective-permute-start | bytes 860168 | tf_op jit(solution)/shard_map/ppermute | solution.py:33
  230.4 5.6 %collective-permute-done.25 = bf16[80,1792]{1,0:T(8,128)(2,1)} collective-permute-done((bf16[80,1792]{1,0:T(8,128)(2,1)}, bf16[80,1792]{1,0:T(8,128)(2,1)}, u32[]{:S(2)}, u32[]{:S(2)}) %collective-permute-start.25) | collective-permute-done | bytes 286752 | tf_op jit(solution)/shard_map/ppermute | solution.py:33
  235.9 4.9 %collective-permute-done.24 = bf16[80,1792]{1,0:T(8,128)(2,1)} collective-permute-done((bf16[80,1792]{1,0:T(8,128)(2,1)S(1)}, bf16[80,1792]{1,0:T(8,128)(2,1)}, u32[]{:S(2)}, u32[]{:S(2)}) %collective-permute-start.24) | collective-permute-done | bytes 286752 | tf_op jit(solution)/shard_map/ppermute | solution.py:33
  240.9 3.0 %collective-permute-start.29 = (bf16[64,1792]{1,0:T(8,128)(2,1)S(1)}, bf16[64,1792]{1,0:T(8,128)(2,1)S(1)}, u32[]{:S(2)}, u32[]{:S(2)}) collective-permute-start(bf16[64,1792]{1,0:T(8,128)(2,1)S(1)} %pad_maximum_fusion.31), channel_id=1, source_target_pairs={{0,18},{1,19},{2,16},{3,17},{4,22},{5,23},{6,20},{7,21},{8,26},{9,... | collective-permute-start | bytes 688136 | tf_op jit(solution)/shard_map/ppermute | solution.py:33
  243.9 1.8 collective-permute-start.28
  247.0 8.1 %collective-permute-done.30 = bf16[64,1792]{1,0:T(8,128)(2,1)S(1)} collective-permute-done((bf16[64,1792]{1,0:T(8,128)(2,1)S(1)}, bf16[64,1792]{1,0:T(8,128)(2,1)S(1)}, u32[]{:S(2)}, u32[]{:S(2)}) %collective-permute-start.30) | collective-permute-done | bytes 229408 | tf_op jit(solution)/shard_map/ppermute | solution.py:33
  (154 shorter events, 44.9 us)
Async XLA Ops:
  6.2 21.2 %collective-permute-start = (bf16[144,1792]{1,0:T(8,128)(2,1)}, bf16[144,1792]{1,0:T(8,128)(2,1)S(1)}, u32[]{:S(2)}, u32[]{:S(2)}) collective-permute-start(bf16[144,1792]{1,0:T(8,128)(2,1)} %convolution_convert_fusion.4), channel_id=1, source_target_pairs={{0,1},{1,2},{2,3},{3,0},{4,5},{5,6},{6,7},{7,4},{8,9},{9,10},{10,1... | collective-permute-start | bytes 1548296 | tf_op jit(solution)/shard_map/ppermute | solution.py:21
  9.4 23.8 %collective-permute-start.1 = (bf16[144,1792]{1,0:T(8,128)(2,1)}, bf16[144,1792]{1,0:T(8,128)(2,1)S(1)}, u32[]{:S(2)}, u32[]{:S(2)}) collective-permute-start(bf16[144,1792]{1,0:T(8,128)(2,1)} %convolution_convert_fusion.3), channel_id=1, source_target_pairs={{0,2},{1,3},{2,0},{3,1},{4,6},{5,7},{6,4},{7,5},{8,10},{9,11},{10,... | collective-permute-start | bytes 1548296 | tf_op jit(solution)/shard_map/ppermute | solution.py:21
  13.0 20.9 %collective-permute-start.2 = (bf16[144,1792]{1,0:T(8,128)(2,1)}, bf16[144,1792]{1,0:T(8,128)(2,1)}, u32[]{:S(2)}, u32[]{:S(2)}) collective-permute-start(bf16[144,1792]{1,0:T(8,128)(2,1)} %convolution_convert_fusion.2), channel_id=1, source_target_pairs={{0,3},{1,0},{2,1},{3,2},{4,7},{5,4},{6,5},{7,6},{8,11},{9,8},{10,9... | collective-permute-start | bytes 1548296 | tf_op jit(solution)/shard_map/ppermute | solution.py:21
  14.1 6.0 %copy-start.8 = (f32[4,1,32]{2,1,0:T(1,128)S(1)}, f32[4,1,32]{2,1,0:T(1,128)}, u32[]{:S(2)}) copy-start(f32[4,1,32]{2,1,0:T(1,128)} %param.9) | copy-start | bytes 1540
  14.1 58.5 %all-to-all-start = ((bf16[4,1792,256]{2,1,0:T(8,128)(2,1)}), bf16[4,1792,256]{2,1,0:T(8,128)(2,1)}, u32[]{:S(2)}, u32[]{:S(2)}) async-start(bf16[4,1792,256]{2,1,0:T(8,128)(2,1)} %bitcast.175), calls=%async_computation | async-start | bytes 7340032 | tf_op jit(solution)/shard_map/all_to_all | solution.py:70
  34.9 12.5 %collective-permute-start.4 = (bf16[4,40,1792]{2,1,0:T(8,128)(2,1)S(1)}, bf16[4,40,1792]{2,1,0:T(8,128)(2,1)S(1)}, u32[]{:S(2)}, u32[]{:S(2)}) collective-permute-start(bf16[4,40,1792]{2,1,0:T(8,128)(2,1)S(1)} %pad_maximum_fusion.10), channel_id=1, source_target_pairs={{0,8},{1,9},{2,10},{3,11},{4,12},{5,13},{6,14},{7,15},{8,0},{9,1},... | collective-permute-start | bytes 1720328 | tf_op jit(solution)/shard_map/ppermute | solution.py:21
  38.3 25.7 %collective-permute-start.3 = (bf16[4,40,1792]{2,1,0:T(8,128)(2,1)S(1)}, bf16[4,40,1792]{2,1,0:T(8,128)(2,1)S(1)}, u32[]{:S(2)}, u32[]{:S(2)}) collective-permute-start(bf16[4,40,1792]{2,1,0:T(8,128)(2,1)S(1)} %get-tuple-element.48), channel_id=1, source_target_pairs={{0,4},{1,5},{2,6},{3,7},{4,8},{5,9},{6,10},{7,11},{8,12},{9,13},{1... | collective-permute-start | bytes 1720328 | tf_op jit(solution)/shard_map/ppermute | solution.py:21
  38.8 25.2 %collective-permute-start.5 = (bf16[4,40,1792]{2,1,0:T(8,128)(2,1)S(1)}, bf16[4,40,1792]{2,1,0:T(8,128)(2,1)S(1)}, u32[]{:S(2)}, u32[]{:S(2)}) collective-permute-start(bf16[4,40,1792]{2,1,0:T(8,128)(2,1)S(1)} %get-tuple-element.49), channel_id=1, source_target_pairs={{0,12},{1,13},{2,14},{3,15},{4,0},{5,1},{6,2},{7,3},{8,4},{9,5},{1... | collective-permute-start | bytes 1720328 | tf_op jit(solution)/shard_map/ppermute | solution.py:21
  64.0 4.1 %copy-start.7 = (bf16[1,32,1792]{2,1,0:T(8,128)(2,1)S(1)}, bf16[1,32,1792]{2,1,0:T(8,128)(2,1)}, u32[]{:S(2)}) copy-start(bf16[1,32,1792]{2,1,0:T(8,128)(2,1)} %get-tuple-element.69) | copy-start | bytes 344068
  65.7 2.5 copy-start
  65.7 3.8 %collective-permute-start.7 = (f32[2,128]{1,0:T(2,128)S(1)}, f32[2,128]{1,0:T(2,128)S(1)}, u32[]{:S(2)}, u32[]{:S(2)}) collective-permute-start(f32[2,128]{1,0:T(2,128)S(1)} %pad_maximum_fusion.33), channel_id=1, source_target_pairs={{0,16},{1,17},{2,18},{3,19},{4,20},{5,21},{6,22},{7,23},{8,24},{9,... | collective-permute-start | bytes 3080 | tf_op jit(solution)/shard_map/ppermute | solution.py:33
  68.2 78.4 %collective-permute-start.6 = (bf16[128,7168]{1,0:T(8,128)(2,1)S(1)}, bf16[128,7168]{1,0:T(8,128)(2,1)}, u32[]{:S(2)}, u32[]{:S(2)}) collective-permute-start(bf16[128,7168]{1,0:T(8,128)(2,1)S(1)} %bitcast.167), channel_id=1, source_target_pairs={{0,16},{1,17},{2,18},{3,19},{4,20},{5,21},{6,22},{7,23},{8,24},{9,... | collective-permute-start | bytes 5505032 | tf_op jit(solution)/shard_map/ppermute | solution.py:33
  72.6 78.7 %all-to-all-start.1 = ((bf16[4,256,1792]{1,2,0:T(8,128)(2,1)}), bf16[4,256,1792]{1,2,0:T(8,128)(2,1)}, u32[]{:S(2)}, u32[]{:S(2)}) async-start(bf16[4,256,1792]{1,2,0:T(8,128)(2,1)} %bitcast.166), calls=%async_computation.1 | async-start | bytes 7340032 | tf_op jit(solution)/shard_map/all_to_all | solution.py:70
  77.4 2.8 %copy-start.1 = (bf16[4,4,40,1792]{3,2,1,0:T(8,128)(2,1)S(1)}, bf16[4,4,40,1792]{3,2,1,0:T(8,128)(2,1)}, u32[]{:S(2)}) copy-start(bf16[4,4,40,1792]{3,2,1,0:T(8,128)(2,1)} %pad_maximum_fusion.1) | copy-start | bytes 6881284
  82.3 24.0 %collective-permute-start.9 = (bf16[4,32,1792]{2,1,0:T(8,128)(2,1)S(1)}, bf16[4,32,1792]{2,1,0:T(8,128)(2,1)S(1)}, u32[]{:S(2)}, u32[]{:S(2)}) collective-permute-start(bf16[4,32,1792]{2,1,0:T(8,128)(2,1)S(1)} %get-tuple-element.20), channel_id=1, source_target_pairs={{0,8},{1,9},{2,10},{3,11},{4,12},{5,13},{6,14},{7,15},{8,0},{9,1},... | collective-permute-start | bytes 1376264 | tf_op jit(solution)/shard_map/ppermute | solution.py:21
  85.3 20.9 %collective-permute-start.8 = (bf16[4,32,1792]{2,1,0:T(8,128)(2,1)S(1)}, bf16[4,32,1792]{2,1,0:T(8,128)(2,1)S(1)}, u32[]{:S(2)}, u32[]{:S(2)}) collective-permute-start(bf16[4,32,1792]{2,1,0:T(8,128)(2,1)S(1)} %get-tuple-element.50), channel_id=1, source_target_pairs={{0,4},{1,5},{2,6},{3,7},{4,8},{5,9},{6,10},{7,11},{8,12},{9,13},{1... | collective-permute-start | bytes 1376264 | tf_op jit(solution)/shard_map/ppermute | solution.py:21
  85.8 20.4 %collective-permute-start.10 = (bf16[4,32,1792]{2,1,0:T(8,128)(2,1)S(1)}, bf16[4,32,1792]{2,1,0:T(8,128)(2,1)S(1)}, u32[]{:S(2)}, u32[]{:S(2)}) collective-permute-start(bf16[4,32,1792]{2,1,0:T(8,128)(2,1)S(1)} %get-tuple-element.51), channel_id=1, source_target_pairs={{0,12},{1,13},{2,14},{3,15},{4,0},{5,1},{6,2},{7,3},{8,4},{9,5},{1... | collective-permute-start | bytes 1376264 | tf_op jit(solution)/shard_map/ppermute | solution.py:21
  110.3 23.4 %collective-permute-start.11 = (bf16[1152,256]{1,0:T(8,128)(2,1)S(1)}, bf16[1152,256]{1,0:T(8,128)(2,1)S(1)}, u32[]{:S(2)}, u32[]{:S(2)}) collective-permute-start(bf16[1152,256]{1,0:T(8,128)(2,1)S(1)} %pad_maximum_fusion.6), channel_id=1, source_target_pairs={{0,3},{1,0},{2,1},{3,2},{4,7},{5,4},{6,5},{7,6},{8,11},{9,8},{10,9... | collective-permute-start | bytes 1769480 | tf_op jit(solution)/shard_map/ppermute | solution.py:21
  115.0 18.7 %collective-permute-start.12 = (bf16[1152,256]{1,0:T(8,128)(2,1)S(1)}, bf16[1152,256]{1,0:T(8,128)(2,1)S(1)}, u32[]{:S(2)}, u32[]{:S(2)}) collective-permute-start(bf16[1152,256]{1,0:T(8,128)(2,1)S(1)} %pad_maximum_fusion.7), channel_id=1, source_target_pairs={{0,2},{1,3},{2,0},{3,1},{4,6},{5,7},{6,4},{7,5},{8,10},{9,11},{10,... | collective-permute-start | bytes 1769480 | tf_op jit(solution)/shard_map/ppermute | solution.py:21
  116.7 29.6 %collective-permute-start.13 = (bf16[1152,256]{1,0:T(8,128)(2,1)S(1)}, bf16[1152,256]{1,0:T(8,128)(2,1)S(1)}, u32[]{:S(2)}, u32[]{:S(2)}) collective-permute-start(bf16[1152,256]{1,0:T(8,128)(2,1)S(1)} %pad_maximum_fusion.8), channel_id=1, source_target_pairs={{0,1},{1,2},{2,3},{3,0},{4,5},{5,6},{6,7},{7,4},{8,9},{9,10},{10,1... | collective-permute-start | bytes 1769480 | tf_op jit(solution)/shard_map/ppermute | solution.py:21
  147.8 30.4 %collective-permute-start.14 = (bf16[640,256]{1,0:T(8,128)(2,1)}, bf16[640,256]{1,0:T(8,128)(2,1)}, u32[]{:S(2)}, u32[]{:S(2)}) collective-permute-start(bf16[640,256]{1,0:T(8,128)(2,1)} %bitcast.48), channel_id=1, source_target_pairs={{0,1},{1,2},{2,3},{3,0},{4,5},{5,6},{6,7},{7,4},{8,9},{9,10},{10,1... | collective-permute-start | bytes 983048 | tf_op jit(solution)/shard_map/ppermute | solution.py:21
  148.6 29.6 %collective-permute-start.16 = (bf16[640,256]{1,0:T(8,128)(2,1)}, bf16[640,256]{1,0:T(8,128)(2,1)}, u32[]{:S(2)}, u32[]{:S(2)}) collective-permute-start(bf16[640,256]{1,0:T(8,128)(2,1)} %bitcast.50), channel_id=1, source_target_pairs={{0,3},{1,0},{2,1},{3,2},{4,7},{5,4},{6,5},{7,6},{8,11},{9,8},{10,9... | collective-permute-start | bytes 983048 | tf_op jit(solution)/shard_map/ppermute | solution.py:21
  152.1 11.7 %collective-permute-start.15 = (bf16[640,256]{1,0:T(8,128)(2,1)}, bf16[640,256]{1,0:T(8,128)(2,1)}, u32[]{:S(2)}, u32[]{:S(2)}) collective-permute-start(bf16[640,256]{1,0:T(8,128)(2,1)} %bitcast.49), channel_id=1, source_target_pairs={{0,2},{1,3},{2,0},{3,1},{4,6},{5,7},{6,4},{7,5},{8,10},{9,11},{10,... | collective-permute-start | bytes 983048 | tf_op jit(solution)/shard_map/ppermute | solution.py:21
  160.1 18.1 %copy-start.5 = (bf16[1,256,1792]{2,1,0:T(8,128)(2,1)}, bf16[1,256,1792]{2,1,0:T(8,128)(2,1)S(1)}, u32[]{:S(2)}) copy-start(bf16[1,256,1792]{2,1,0:T(8,128)(2,1)S(1)} %copy.10) | copy-start | bytes 2752516
  160.1 18.1 %copy-start.3 = (bf16[1,256,1792]{2,1,0:T(8,128)(2,1)S(1)}, bf16[1,256,1792]{2,1,0:T(8,128)(2,1)}, u32[]{:S(2)}) copy-start(bf16[1,256,1792]{2,1,0:T(8,128)(2,1)} %copy.7) | copy-start | bytes 2752516
  160.1 18.1 %copy-start.4 = (bf16[1,256,1792]{2,1,0:T(8,128)(2,1)S(1)}, bf16[1,256,1792]{2,1,0:T(8,128)(2,1)}, u32[]{:S(2)}) copy-start(bf16[1,256,1792]{2,1,0:T(8,128)(2,1)} %copy.8) | copy-start | bytes 2752516
  163.9 22.1 %collective-permute-start.21 = (bf16[512,256]{1,0:T(8,128)(2,1)S(1)}, bf16[512,256]{1,0:T(8,128)(2,1)S(1)}, u32[]{:S(2)}, u32[]{:S(2)}) collective-permute-start(bf16[512,256]{1,0:T(8,128)(2,1)S(1)} %bitcast.215), channel_id=1, source_target_pairs={{0,1},{1,2},{2,3},{3,0},{4,5},{5,6},{6,7},{7,4},{8,9},{9,10},{10,1... | collective-permute-start | bytes 786440 | tf_op jit(solution)/shard_map/ppermute | solution.py:21
  165.6 22.0 %collective-permute-start.22 = (bf16[512,256]{1,0:T(8,128)(2,1)S(1)}, bf16[512,256]{1,0:T(8,128)(2,1)S(1)}, u32[]{:S(2)}, u32[]{:S(2)}) collective-permute-start(bf16[512,256]{1,0:T(8,128)(2,1)S(1)} %bitcast.216), channel_id=1, source_target_pairs={{0,2},{1,3},{2,0},{3,1},{4,6},{5,7},{6,4},{7,5},{8,10},{9,11},{10,... | collective-permute-start | bytes 786440 | tf_op jit(solution)/shard_map/ppermute | solution.py:21
  168.0 19.6 %collective-permute-start.23 = (bf16[512,256]{1,0:T(8,128)(2,1)S(1)}, bf16[512,256]{1,0:T(8,128)(2,1)S(1)}, u32[]{:S(2)}, u32[]{:S(2)}) collective-permute-start(bf16[512,256]{1,0:T(8,128)(2,1)S(1)} %bitcast.217), channel_id=1, source_target_pairs={{0,3},{1,0},{2,1},{3,2},{4,7},{5,4},{6,5},{7,6},{8,11},{9,8},{10,9... | collective-permute-start | bytes 786440 | tf_op jit(solution)/shard_map/ppermute | solution.py:21
  182.0 5.7 %copy-start.6 = (bf16[1,256,1792]{2,1,0:T(8,128)(2,1)S(1)}, bf16[1,256,1792]{2,1,0:T(8,128)(2,1)}, u32[]{:S(2)}) copy-start(bf16[1,256,1792]{2,1,0:T(8,128)(2,1)} %copy-done.5) | copy-start | bytes 2752516
  183.2 13.3 %collective-permute-start.17 = (bf16[4,40,1792]{2,1,0:T(8,128)(2,1)}, bf16[4,40,1792]{2,1,0:T(8,128)(2,1)}, u32[]{:S(2)}, u32[]{:S(2)}) collective-permute-start(bf16[4,40,1792]{2,1,0:T(8,128)(2,1)} %bitcast.58), channel_id=1, source_target_pairs={{0,12},{1,13},{2,14},{3,15},{4,0},{5,1},{6,2},{7,3},{8,4},{9,5},{1... | collective-permute-start | bytes 1720328 | tf_op jit(solution)/shard_map/ppermute | solution.py:21
  186.0 13.7 %collective-permute-start.18 = (bf16[4,40,1792]{2,1,0:T(8,128)(2,1)}, bf16[4,40,1792]{2,1,0:T(8,128)(2,1)}, u32[]{:S(2)}, u32[]{:S(2)}) collective-permute-start(bf16[4,40,1792]{2,1,0:T(8,128)(2,1)} %bitcast.59), channel_id=1, source_target_pairs={{0,4},{1,5},{2,6},{3,7},{4,8},{5,9},{6,10},{7,11},{8,12},{9,13},{1... | collective-permute-start | bytes 1720328 | tf_op jit(solution)/shard_map/ppermute | solution.py:21
  186.0 24.0 %collective-permute-start.19 = (bf16[4,40,1792]{2,1,0:T(8,128)(2,1)}, bf16[4,40,1792]{2,1,0:T(8,128)(2,1)}, u32[]{:S(2)}, u32[]{:S(2)}) collective-permute-start(bf16[4,40,1792]{2,1,0:T(8,128)(2,1)} %bitcast.61), channel_id=1, source_target_pairs={{0,8},{1,9},{2,10},{3,11},{4,12},{5,13},{6,14},{7,15},{8,0},{9,1},... | collective-permute-start | bytes 1720328 | tf_op jit(solution)/shard_map/ppermute | solution.py:21
  191.3 38.3 %all-to-all-start.2 = ((bf16[4,4,32,1792]{3,2,1,0:T(8,128)(2,1)}), bf16[4,4,32,1792]{3,2,1,0:T(8,128)(2,1)S(1)}, u32[]{:S(2)}, u32[]{:S(2)}) async-start(bf16[4,4,32,1792]{3,2,1,0:T(8,128)(2,1)} %pad_maximum_fusion.3), calls=%async_computation.2 | async-start | bytes 3670016 | tf_op jit(solution)/shard_map/all_to_all | solution.py:70
  211.8 18.5 %collective-permute-start.26 = (bf16[80,1792]{1,0:T(8,128)(2,1)S(1)}, bf16[80,1792]{1,0:T(8,128)(2,1)}, u32[]{:S(2)}, u32[]{:S(2)}) collective-permute-start(bf16[80,1792]{1,0:T(8,128)(2,1)S(1)} %pad_maximum_fusion.22), channel_id=1, source_target_pairs={{0,17},{1,18},{2,19},{3,16},{4,21},{5,22},{6,23},{7,20},{8,25},{9,... | collective-permute-start | bytes 860168 | tf_op jit(solution)/shard_map/ppermute | solution.py:33
  224.2 11.7 %collective-permute-start.25 = (bf16[80,1792]{1,0:T(8,128)(2,1)}, bf16[80,1792]{1,0:T(8,128)(2,1)}, u32[]{:S(2)}, u32[]{:S(2)}) collective-permute-start(bf16[80,1792]{1,0:T(8,128)(2,1)} %pad_maximum_fusion.21), channel_id=1, source_target_pairs={{0,18},{1,19},{2,16},{3,17},{4,22},{5,23},{6,20},{7,21},{8,26},{9,... | collective-permute-start | bytes 860168 | tf_op jit(solution)/shard_map/ppermute | solution.py:33
  224.2 16.6 %collective-permute-start.24 = (bf16[80,1792]{1,0:T(8,128)(2,1)S(1)}, bf16[80,1792]{1,0:T(8,128)(2,1)}, u32[]{:S(2)}, u32[]{:S(2)}) collective-permute-start(bf16[80,1792]{1,0:T(8,128)(2,1)S(1)} %pad_maximum_fusion.20), channel_id=1, source_target_pairs={{0,19},{1,16},{2,17},{3,18},{4,23},{5,20},{6,21},{7,22},{8,27},{9,... | collective-permute-start | bytes 860168 | tf_op jit(solution)/shard_map/ppermute | solution.py:33
  227.5 13.4 %collective-permute-start.20 = (bf16[80,1792]{1,0:T(8,128)(2,1)S(1)}, bf16[80,1792]{1,0:T(8,128)(2,1)S(1)}, u32[]{:S(2)}, u32[]{:S(2)}) collective-permute-start(bf16[80,1792]{1,0:T(8,128)(2,1)S(1)} %pad_maximum_fusion.19), channel_id=1, source_target_pairs={{0,16},{1,17},{2,18},{3,19},{4,20},{5,21},{6,22},{7,23},{8,24},{9,... | collective-permute-start | bytes 860168 | tf_op jit(solution)/shard_map/ppermute | solution.py:33
  240.9 14.3 %collective-permute-start.30 = (bf16[64,1792]{1,0:T(8,128)(2,1)S(1)}, bf16[64,1792]{1,0:T(8,128)(2,1)S(1)}, u32[]{:S(2)}, u32[]{:S(2)}) collective-permute-start(bf16[64,1792]{1,0:T(8,128)(2,1)S(1)} %pad_maximum_fusion.32), channel_id=1, source_target_pairs={{0,17},{1,18},{2,19},{3,16},{4,21},{5,22},{6,23},{7,20},{8,25},{9,... | collective-permute-start | bytes 688136 | tf_op jit(solution)/shard_map/ppermute | solution.py:33
  240.9 14.6 %collective-permute-start.29 = (bf16[64,1792]{1,0:T(8,128)(2,1)S(1)}, bf16[64,1792]{1,0:T(8,128)(2,1)S(1)}, u32[]{:S(2)}, u32[]{:S(2)}) collective-permute-start(bf16[64,1792]{1,0:T(8,128)(2,1)S(1)} %pad_maximum_fusion.31), channel_id=1, source_target_pairs={{0,18},{1,19},{2,16},{3,17},{4,22},{5,23},{6,20},{7,21},{8,26},{9,... | collective-permute-start | bytes 688136 | tf_op jit(solution)/shard_map/ppermute | solution.py:33
  243.9 11.9 %collective-permute-start.28 = (bf16[64,1792]{1,0:T(8,128)(2,1)S(1)}, bf16[64,1792]{1,0:T(8,128)(2,1)S(1)}, u32[]{:S(2)}, u32[]{:S(2)}) collective-permute-start(bf16[64,1792]{1,0:T(8,128)(2,1)S(1)} %pad_maximum_fusion.30), channel_id=1, source_target_pairs={{0,19},{1,16},{2,17},{3,18},{4,23},{5,20},{6,21},{7,22},{8,27},{9,... | collective-permute-start | bytes 688136 | tf_op jit(solution)/shard_map/ppermute | solution.py:33
  245.7 10.4 %collective-permute-start.27 = (bf16[64,1792]{1,0:T(8,128)(2,1)S(1)}, bf16[64,1792]{1,0:T(8,128)(2,1)S(1)}, u32[]{:S(2)}, u32[]{:S(2)}) collective-permute-start(bf16[64,1792]{1,0:T(8,128)(2,1)S(1)} %pad_maximum_fusion.29), channel_id=1, source_target_pairs={{0,16},{1,17},{2,18},{3,19},{4,20},{5,21},{6,22},{7,23},{8,24},{9,... | collective-permute-start | bytes 688136 | tf_op jit(solution)/shard_map/ppermute | solution.py:33
  262.3 1.2 copy-start.2

commit v2 on v0

--- a/solution.py
+++ b/solution.py
@@ -33,10 +33,9 @@
     return lax.ppermute(block, ("pipe", "expert"), pairs)
 
 
-def normalize(tok_rows):
+def inverse_rms(tok_rows):
     widened = tok_rows.astype(jnp.float32)
-    inverse_rms = lax.rsqrt(jnp.mean(widened * widened, axis=-1, keepdims=True) + epsilon)
-    return (widened * inverse_rms).astype(jnp.bfloat16)
+    return lax.rsqrt(jnp.mean(widened * widened, axis=-1, keepdims=True) + epsilon)
 
 
 def slots_of(ids, own):
@@ -96,11 +95,12 @@
     slot = slots_of(route.reshape(count), own)
     lanes = jnp.arange(EXPERTS * ticks * CAP, dtype=jnp.int32)
     table = (lanes[:, None] == slot[None, :]).astype(jnp.bfloat16)
-    normed = normalize(rows)
+    scale = inverse_rms(rows)
 
     from_x = []
     for step in range(SIDE):
-        part = lax.dynamic_slice(normed, (0, quarter(step)), (count, PART))
+        part = lax.dynamic_slice(rows, (0, quarter(step)), (count, PART))
+        part = (part.astype(jnp.float32) * scale).astype(jnp.bfloat16)
         message = jnp.dot(table, part, preferred_element_type=jnp.float32).astype(jnp.bfloat16)
         from_x.append(shift(message, 0, step) if step else message)
 
@@ -140,7 +140,7 @@
         sent = tie(hiddens[c], *gathered[0][1:]) if c else hiddens[c]
         gathered.append([shift(turn(sent, step, CUTS[c]), 0, step) if step else sent for step in range(SIDE)])
 
-    combined = [0.0] * SIDE
+    result = rows_before
     landed = []
     for c in cuts:
         out = 0.0
@@ -165,13 +165,11 @@
         landed = [shift_on(message, -step) for step, message in enumerate(messages)]
         chosen = table[:, starts[c] : starts[c] + EXPERTS * CUTS[c]]
         for step in range(SIDE):
-            combined[step] = combined[step] + jnp.dot(chosen, landed[step], preferred_element_type=jnp.float32)
+            combined = jnp.dot(chosen, landed[step], preferred_element_type=jnp.float32)
+            part = lax.dynamic_slice(result, (0, quarter(step)), (count, PART))
+            updated = part.astype(jnp.float32) + facts_before[1][:, None] * combined
+            result = lax.dynamic_update_slice(result, updated.astype(jnp.bfloat16), (0, quarter(step)))
 
-    result = jnp.zeros((count, D), jnp.bfloat16)
-    for step in range(SIDE):
-        part = lax.dynamic_slice(rows_before, (0, quarter(step)), (count, PART))
-        updated = part.astype(jnp.float32) + facts_before[1][:, None] * combined[step]
-        result = lax.dynamic_update_slice(result, updated.astype(jnp.bfloat16), (0, quarter(step)))
     return result.reshape(tokens.shape)
 
 

time: 264 us -> 261 us (0.989)
  starting transfers between devices: 74.4 us -> 77.8 us
  waiting for transfers between devices: 116 us -> 113 us
    ppermute x10, waiting for transfers between devices: 13.7 us -> 22.5 us  [shift_on(): return lax.ppermute(block, ('pipe', 'expert'), pairs)]
    all_to_all x3, waiting for transfers between devices: 10.3 us -> 1.7 us  [exchange(): lax.all_to_all(pieces, 'expert', 0, 0, axis_index_groups=groups, tiled=True)]
    dot_general x8, matrix products: 6.86 us -> 2.45 us  [per_device(): combined = jnp.dot(chosen, landed[step], preferred_element_type=jnp.float32)]
    ppermute x21, starting transfers between devices: 42.1 us -> 45.6 us  [shift(): return lax.ppermute(block, 'expert', pairs)]
    ppermute x21, waiting for transfers between devices: 91.7 us -> 88.3 us  [shift(): return lax.ppermute(block, 'expert', pairs)]
    dot_general x4, matrix products: 3.64 us -> 6.35 us  [per_device(): jnp.dot(table, part, preferred_element_type=jnp.float32)]
    unnamed x12 -> x11, local copies, waits for them, and re-layouts: 7.74 us -> 7.65 us
  transfers between devices with their start and end apart: 34 -> 34, of which waited for: 18 -> 20; matrix products, arithmetic and copies ran while one was open for 18% -> 20% of each run, Pallas kernels for 0% -> 0%
where the time goes in v2:
time: 261 us; the launch traced here: 257 us
  waiting for transfers between devices  113 us (43%)
  starting transfers between devices  77.8 us (30%)
  matrix products  40.7 us (16%)
  other arithmetic  14 us (5%)
  local copies, waits for them, and re-layouts  10.8 us (4%)
    ppermute x21, waiting for transfers between devices, shift(): return lax.ppermute(block, 'expert', pairs)  88.3 us
    ppermute x21, starting transfers between devices, shift(): return lax.ppermute(block, 'expert', pairs)  45.6 us
    ppermute x10, waiting for transfers between devices, shift_on(): return lax.ppermute(block, ('pipe', 'expert'), pairs)  22.5 us
    ppermute x10, starting transfers between devices, shift_on(): return lax.ppermute(block, ('pipe', 'expert'), pairs)  18.1 us
    dot_general x8, matrix products, per_device(): jnp.dot(received[c], of(ups, -step), preferred_element_type=jnp.float32)  15.9 us
    dot_general x8, matrix products, per_device(): jnp.dot(gathered[c][step], of(downs, -step), preferred_element_type=jnp.f...  15.8 us
    all_to_all x3, starting transfers between devices, exchange(): lax.all_to_all(pieces, 'expert', 0, 0, axis_index_groups=groups, tiled=True)  14 us
    unnamed x11, local copies, waits for them, and re-layouts  7.65 us
  transfers between devices with their start and end apart: 34, of which 20 were waited for; matrix products, arithmetic and copies ran while one was open for 20% of the time, Pallas kernels for 0%

profile of v2, /device:TPU:1, one launch (start us, length us, event | category | flops | bytes accessed | tf_op | source)
XLA Modules:
  0.0 256.7 jit_solution(12896233400265013757)
XLA Ops:
  0.0 2.0 multiply_reduce_fusion
  3.9 3.4 %collective-permute-start.2 = (bf16[144,1792]{1,0:T(8,128)(2,1)S(1)}, bf16[144,1792]{1,0:T(8,128)(2,1)S(1)}, u32[]{:S(2)}, u32[]{:S(2)}) collective-permute-start(bf16[144,1792]{1,0:T(8,128)(2,1)S(1)} %convolution_convert_fusion), channel_id=1, source_target_pairs={{0,3},{1,0},{2,1},{3,2},{4,7},{5,4},{6,5},{7,6},{8,11},{9,8},{10,9... | collective-permute-start | bytes 1548296 | tf_op jit(solution)/shard_map/ppermute | solution.py:21
  9.3 2.2 convolution_convert_fusion.2
  12.1 4.9 %all-to-all-start = ((bf16[4,1792,256]{2,1,0:T(8,128)(2,1)}), bf16[4,1792,256]{2,1,0:T(8,128)(2,1)}, u32[]{:S(2)}, u32[]{:S(2)}) async-start(bf16[4,1792,256]{2,1,0:T(8,128)(2,1)} %bitcast.210), calls=%async_computation | async-start | bytes 7340032 | tf_op jit(solution)/shard_map/all_to_all | solution.py:69
  20.6 5.8 %copy.6 = bf16[1,256,7168]{1,2,0:T(8,128)(2,1)} copy(bf16[1,256,7168]{2,1,0:T(8,128)(2,1)} %param.7) | data formatting | bytes 7340032 | tf_op args[2]
  26.5 8.6 %collective-permute-done = bf16[144,1792]{1,0:T(8,128)(2,1)S(1)} collective-permute-done((bf16[144,1792]{1,0:T(8,128)(2,1)}, bf16[144,1792]{1,0:T(8,128)(2,1)S(1)}, u32[]{:S(2)}, u32[]{:S(2)}) %collective-permute-start) | collective-permute-done | bytes 516128 | tf_op jit(solution)/shard_map/ppermute | solution.py:21
  35.2 2.8 %collective-permute-start.5 = (bf16[4,40,1792]{2,1,0:T(8,128)(2,1)S(1)}, bf16[4,40,1792]{2,1,0:T(8,128)(2,1)S(1)}, u32[]{:S(2)}, u32[]{:S(2)}) collective-permute-start(bf16[4,40,1792]{2,1,0:T(8,128)(2,1)S(1)} %get-tuple-element.43), channel_id=1, source_target_pairs={{0,12},{1,13},{2,14},{3,15},{4,0},{5,1},{6,2},{7,3},{8,4},{9,5},{1... | collective-permute-start | bytes 1720328 | tf_op jit(solution)/shard_map/ppermute | solution.py:21
  39.4 22.5 %collective-permute-done.5 = bf16[4,40,1792]{2,1,0:T(8,128)(2,1)S(1)} collective-permute-done((bf16[4,40,1792]{2,1,0:T(8,128)(2,1)S(1)}, bf16[4,40,1792]{2,1,0:T(8,128)(2,1)S(1)}, u32[]{:S(2)}, u32[]{:S(2)}) %collective-permute-start.5) | collective-permute-done | bytes 573472 | tf_op jit(solution)/shard_map/ppermute | solution.py:21
  62.0 5.1 %collective-permute-done.3 = bf16[4,40,1792]{2,1,0:T(8,128)(2,1)S(1)} collective-permute-done((bf16[4,40,1792]{2,1,0:T(8,128)(2,1)S(1)}, bf16[4,40,1792]{2,1,0:T(8,128)(2,1)S(1)}, u32[]{:S(2)}, u32[]{:S(2)}) %collective-permute-start.3) | collective-permute-done | bytes 573472 | tf_op jit(solution)/shard_map/ppermute | solution.py:21
  67.0 1.8 pad_maximum_fusion
  68.8 1.9 collective-permute-start.7
  73.1 4.8 %all-to-all-start.1 = ((bf16[4,256,1792]{1,2,0:T(8,128)(2,1)}), bf16[4,256,1792]{1,2,0:T(8,128)(2,1)}, u32[]{:S(2)}, u32[]{:S(2)}) async-start(bf16[4,256,1792]{1,2,0:T(8,128)(2,1)} %bitcast.201), calls=%async_computation.1 | async-start | bytes 7340032 | tf_op jit(solution)/shard_map/all_to_all | solution.py:69
  77.9 2.8 %convolution_convert_fusion.4 = bf16[640,256]{1,0:T(8,128)(2,1)S(1)} fusion(bf16[640,1792]{1,0:T(8,128)(2,1)} %bitcast.212, bf16[4,1792,256]{2,1,0:T(8,128)(2,1)} %all-to-all-done, s32[]{:T(128)S(6)} %select_n.294), kind=kOutput, calls=%fused_computation.32 | convolution fusion | flops 587366400 | bytes 3538948 | tf_op jit(solution)/shard_map/dot_general | solution.py:126
  80.8 1.9 convolution_convert_fusion.6
  82.8 3.0 %collective-permute-start.9 = (bf16[4,32,1792]{2,1,0:T(8,128)(2,1)S(1)}, bf16[4,32,1792]{2,1,0:T(8,128)(2,1)S(1)}, u32[]{:S(2)}, u32[]{:S(2)}) collective-permute-start(bf16[4,32,1792]{2,1,0:T(8,128)(2,1)S(1)} %get-tuple-element.19), channel_id=1, source_target_pairs={{0,8},{1,9},{2,10},{3,11},{4,12},{5,13},{6,14},{7,15},{8,0},{9,1},... | collective-permute-start | bytes 1376264 | tf_op jit(solution)/shard_map/ppermute | solution.py:21
  87.6 1.9 convolution_convert_fusion.5
  89.7 16.2 %collective-permute-done.10 = bf16[4,32,1792]{2,1,0:T(8,128)(2,1)S(1)} collective-permute-done((bf16[4,32,1792]{2,1,0:T(8,128)(2,1)S(1)}, bf16[4,32,1792]{2,1,0:T(8,128)(2,1)S(1)}, u32[]{:S(2)}, u32[]{:S(2)}) %collective-permute-start.10) | collective-permute-done | bytes 458784 | tf_op jit(solution)/shard_map/ppermute | solution.py:21
  106.9 1.8 convolution_convert_fusion.7
  108.8 1.8 convolution_convert_fusion.9
  111.8 1.8 convolution_convert_fusion.8
  113.7 2.6 %collective-permute-start.12 = (bf16[1152,256]{1,0:T(8,128)(2,1)S(1)}, bf16[1152,256]{1,0:T(8,128)(2,1)S(1)}, u32[]{:S(2)}, u32[]{:S(2)}) collective-permute-start(bf16[1152,256]{1,0:T(8,128)(2,1)S(1)} %pad_maximum_fusion.4), channel_id=1, source_target_pairs={{0,2},{1,3},{2,0},{3,1},{4,6},{5,7},{6,4},{7,5},{8,10},{9,11},{10,... | collective-permute-start | bytes 1769480 | tf_op jit(solution)/shard_map/ppermute | solution.py:21
  117.6 1.9 fusion.47
  119.6 1.8 fusion.45
  121.4 16.0 %collective-permute-done.13 = bf16[1152,256]{1,0:T(8,128)(2,1)S(1)} collective-permute-done((bf16[1152,256]{1,0:T(8,128)(2,1)S(1)}, bf16[1152,256]{1,0:T(8,128)(2,1)S(1)}, u32[]{:S(2)}, u32[]{:S(2)}) %collective-permute-start.13) | collective-permute-done | bytes 589856 | tf_op jit(solution)/shard_map/ppermute | solution.py:21
  137.4 6.1 %collective-permute-done.12 = bf16[1152,256]{1,0:T(8,128)(2,1)S(1)} collective-permute-done((bf16[1152,256]{1,0:T(8,128)(2,1)S(1)}, bf16[1152,256]{1,0:T(8,128)(2,1)S(1)}, u32[]{:S(2)}, u32[]{:S(2)}) %collective-permute-start.12) | collective-permute-done | bytes 589856 | tf_op jit(solution)/shard_map/ppermute | solution.py:21
  145.7 2.8 %collective-permute-start.15 = (bf16[640,256]{1,0:T(8,128)(2,1)}, bf16[640,256]{1,0:T(8,128)(2,1)S(1)}, u32[]{:S(2)}, u32[]{:S(2)}) collective-permute-start(bf16[640,256]{1,0:T(8,128)(2,1)} %bitcast.53), channel_id=1, source_target_pairs={{0,2},{1,3},{2,0},{3,1},{4,6},{5,7},{6,4},{7,5},{8,10},{9,11},{10,... | collective-permute-start | bytes 983048 | tf_op jit(solution)/shard_map/ppermute | solution.py:21
  152.8 2.0 fusion.37
  154.8 8.8 %collective-permute-done.14 = bf16[640,256]{1,0:T(8,128)(2,1)S(1)} collective-permute-done((bf16[640,256]{1,0:T(8,128)(2,1)}, bf16[640,256]{1,0:T(8,128)(2,1)S(1)}, u32[]{:S(2)}, u32[]{:S(2)}) %collective-permute-start.14) | collective-permute-done | bytes 327712 | tf_op jit(solution)/shard_map/ppermute | solution.py:21
  164.5 2.0 fusion.29
  166.5 2.0 fusion.33
  168.5 2.3 add_convert_fusion
  171.9 11.0 %collective-permute-start.18 = (bf16[4,40,1792]{2,1,0:T(8,128)(2,1)}, bf16[4,40,1792]{2,1,0:T(8,128)(2,1)}, u32[]{:S(2)}, u32[]{:S(2)}) collective-permute-start(bf16[4,40,1792]{2,1,0:T(8,128)(2,1)} %bitcast.59), channel_id=1, source_target_pairs={{0,4},{1,5},{2,6},{3,7},{4,8},{5,9},{6,10},{7,11},{8,12},{9,13},{1... | collective-permute-start | bytes 1720328 | tf_op jit(solution)/shard_map/ppermute | solution.py:21
  186.0 2.7 %collective-permute-start.25 = (bf16[512,256]{1,0:T(8,128)(2,1)S(1)}, bf16[512,256]{1,0:T(8,128)(2,1)S(1)}, u32[]{:S(2)}, u32[]{:S(2)}) collective-permute-start(bf16[512,256]{1,0:T(8,128)(2,1)S(1)} %bitcast.244), channel_id=1, source_target_pairs={{0,2},{1,3},{2,0},{3,1},{4,6},{5,7},{6,4},{7,5},{8,10},{9,11},{10,... | collective-permute-start | bytes 786440 | tf_op jit(solution)/shard_map/ppermute | solution.py:21
  190.0 1.9 fusion.35
  193.2 4.1 %collective-permute-start.26 = (bf16[512,256]{1,0:T(8,128)(2,1)S(1)}, bf16[512,256]{1,0:T(8,128)(2,1)S(1)}, u32[]{:S(2)}, u32[]{:S(2)}) collective-permute-start(bf16[512,256]{1,0:T(8,128)(2,1)S(1)} %bitcast.243), channel_id=1, source_target_pairs={{0,3},{1,0},{2,1},{3,2},{4,7},{5,4},{6,5},{7,6},{8,11},{9,8},{10,9... | collective-permute-start | bytes 786440 | tf_op jit(solution)/shard_map/ppermute | solution.py:21
  197.3 1.9 fusion.27
  200.6 1.9 fusion.31
  202.4 2.0 add_convert_fusion.1
  206.1 4.4 %all-to-all-start.2 = ((bf16[4,4,32,1792]{3,2,1,0:T(8,128)(2,1)}), bf16[4,4,32,1792]{3,2,1,0:T(8,128)(2,1)}, u32[]{:S(2)}, u32[]{:S(2)}) async-start(bf16[4,4,32,1792]{3,2,1,0:T(8,128)(2,1)} %pad_maximum_fusion.2), calls=%async_computation.2 | async-start | bytes 3670016 | tf_op jit(solution)/shard_map/all_to_all | solution.py:69
  210.5 1.7 fusion.15
  212.4 4.1 %collective-permute-start.20 = (bf16[80,1792]{1,0:T(8,128)(2,1)S(1)}, bf16[80,1792]{1,0:T(8,128)(2,1)S(1)}, u32[]{:S(2)}, u32[]{:S(2)}) collective-permute-start(bf16[80,1792]{1,0:T(8,128)(2,1)S(1)} %pad_maximum_fusion.16), channel_id=1, source_target_pairs={{0,16},{1,17},{2,18},{3,19},{4,20},{5,21},{6,22},{7,23},{8,24},{9,... | collective-permute-start | bytes 860168 | tf_op jit(solution)/shard_map/ppermute | solution.py:33
  216.5 2.0 collective-permute-start.21
  218.5 3.1 %collective-permute-start.22 = (bf16[80,1792]{1,0:T(8,128)(2,1)S(1)}, bf16[80,1792]{1,0:T(8,128)(2,1)S(1)}, u32[]{:S(2)}, u32[]{:S(2)}) collective-permute-start(bf16[80,1792]{1,0:T(8,128)(2,1)S(1)} %pad_maximum_fusion.18), channel_id=1, source_target_pairs={{0,18},{1,19},{2,16},{3,17},{4,22},{5,23},{6,20},{7,21},{8,26},{9,... | collective-permute-start | bytes 860168 | tf_op jit(solution)/shard_map/ppermute | solution.py:33
  223.5 3.0 %collective-permute-done.22 = bf16[80,1792]{1,0:T(8,128)(2,1)S(1)} collective-permute-done((bf16[80,1792]{1,0:T(8,128)(2,1)S(1)}, bf16[80,1792]{1,0:T(8,128)(2,1)S(1)}, u32[]{:S(2)}, u32[]{:S(2)}) %collective-permute-start.22) | collective-permute-done | bytes 286752 | tf_op jit(solution)/shard_map/ppermute | solution.py:33
  226.7 8.8 %collective-permute-done.23 = bf16[80,1792]{1,0:T(8,128)(2,1)S(1)} collective-permute-done((bf16[80,1792]{1,0:T(8,128)(2,1)S(1)}, bf16[80,1792]{1,0:T(8,128)(2,1)S(1)}, u32[]{:S(2)}, u32[]{:S(2)}) %collective-permute-start.23) | collective-permute-done | bytes 286752 | tf_op jit(solution)/shard_map/ppermute | solution.py:33
  235.8 1.9 convert_element_type.261
  240.5 2.9 %collective-permute-start.29 = (bf16[64,1792]{1,0:T(8,128)(2,1)S(1)}, bf16[64,1792]{1,0:T(8,128)(2,1)S(1)}, u32[]{:S(2)}, u32[]{:S(2)}) collective-permute-start(bf16[64,1792]{1,0:T(8,128)(2,1)S(1)} %pad_maximum_fusion.28), channel_id=1, source_target_pairs={{0,18},{1,19},{2,16},{3,17},{4,22},{5,23},{6,20},{7,21},{8,26},{9,... | collective-permute-start | bytes 688136 | tf_op jit(solution)/shard_map/ppermute | solution.py:33
  247.8 7.2 %collective-permute-done.30 = bf16[64,1792]{1,0:T(8,128)(2,1)S(1)} collective-permute-done((bf16[64,1792]{1,0:T(8,128)(2,1)S(1)}, bf16[64,1792]{1,0:T(8,128)(2,1)S(1)}, u32[]{:S(2)}, u32[]{:S(2)}) %collective-permute-start.30) | collective-permute-done | bytes 229408 | tf_op jit(solution)/shard_map/ppermute | solution.py:33
  (144 shorter events, 46.2 us)
Async XLA Ops:
  0.0 2.1 copy-start.2
  3.9 22.5 %collective-permute-start.2 = (bf16[144,1792]{1,0:T(8,128)(2,1)S(1)}, bf16[144,1792]{1,0:T(8,128)(2,1)S(1)}, u32[]{:S(2)}, u32[]{:S(2)}) collective-permute-start(bf16[144,1792]{1,0:T(8,128)(2,1)S(1)} %convolution_convert_fusion), channel_id=1, source_target_pairs={{0,3},{1,0},{2,1},{3,2},{4,7},{5,4},{6,5},{7,6},{8,11},{9,8},{10,9... | collective-permute-start | bytes 1548296 | tf_op jit(solution)/shard_map/ppermute | solution.py:21
  8.7 17.7 %collective-permute-start.1 = (bf16[144,1792]{1,0:T(8,128)(2,1)S(1)}, bf16[144,1792]{1,0:T(8,128)(2,1)S(1)}, u32[]{:S(2)}, u32[]{:S(2)}) collective-permute-start(bf16[144,1792]{1,0:T(8,128)(2,1)S(1)} %convolution_convert_fusion.1), channel_id=1, source_target_pairs={{0,2},{1,3},{2,0},{3,1},{4,6},{5,7},{6,4},{7,5},{8,10},{9,11},{10,... | collective-permute-start | bytes 1548296 | tf_op jit(solution)/shard_map/ppermute | solution.py:21
  11.5 23.5 %collective-permute-start = (bf16[144,1792]{1,0:T(8,128)(2,1)}, bf16[144,1792]{1,0:T(8,128)(2,1)S(1)}, u32[]{:S(2)}, u32[]{:S(2)}) collective-permute-start(bf16[144,1792]{1,0:T(8,128)(2,1)} %convolution_convert_fusion.2), channel_id=1, source_target_pairs={{0,1},{1,2},{2,3},{3,0},{4,5},{5,6},{6,7},{7,4},{8,9},{9,10},{10,1... | collective-permute-start | bytes 1548296 | tf_op jit(solution)/shard_map/ppermute | solution.py:21
  12.1 6.9 %copy-start.3 = (f32[4,1,32]{2,1,0:T(1,128)S(1)}, f32[4,1,32]{2,1,0:T(1,128)}, u32[]{:S(2)}) copy-start(f32[4,1,32]{2,1,0:T(1,128)} %param.9) | copy-start | bytes 1540
  12.1 61.0 %all-to-all-start = ((bf16[4,1792,256]{2,1,0:T(8,128)(2,1)}), bf16[4,1792,256]{2,1,0:T(8,128)(2,1)}, u32[]{:S(2)}, u32[]{:S(2)}) async-start(bf16[4,1792,256]{2,1,0:T(8,128)(2,1)} %bitcast.210), calls=%async_computation | async-start | bytes 7340032 | tf_op jit(solution)/shard_map/all_to_all | solution.py:69
  35.2 26.7 %collective-permute-start.5 = (bf16[4,40,1792]{2,1,0:T(8,128)(2,1)S(1)}, bf16[4,40,1792]{2,1,0:T(8,128)(2,1)S(1)}, u32[]{:S(2)}, u32[]{:S(2)}) collective-permute-start(bf16[4,40,1792]{2,1,0:T(8,128)(2,1)S(1)} %get-tuple-element.43), channel_id=1, source_target_pairs={{0,12},{1,13},{2,14},{3,15},{4,0},{5,1},{6,2},{7,3},{8,4},{9,5},{1... | collective-permute-start | bytes 1720328 | tf_op jit(solution)/shard_map/ppermute | solution.py:21
  38.1 23.8 %collective-permute-start.4 = (bf16[4,40,1792]{2,1,0:T(8,128)(2,1)S(1)}, bf16[4,40,1792]{2,1,0:T(8,128)(2,1)S(1)}, u32[]{:S(2)}, u32[]{:S(2)}) collective-permute-start(bf16[4,40,1792]{2,1,0:T(8,128)(2,1)S(1)} %pad_maximum_fusion.7), channel_id=1, source_target_pairs={{0,8},{1,9},{2,10},{3,11},{4,12},{5,13},{6,14},{7,15},{8,0},{9,1},... | collective-permute-start | bytes 1720328 | tf_op jit(solution)/shard_map/ppermute | solution.py:21
  38.6 28.4 %collective-permute-start.3 = (bf16[4,40,1792]{2,1,0:T(8,128)(2,1)S(1)}, bf16[4,40,1792]{2,1,0:T(8,128)(2,1)S(1)}, u32[]{:S(2)}, u32[]{:S(2)}) collective-permute-start(bf16[4,40,1792]{2,1,0:T(8,128)(2,1)S(1)} %get-tuple-element.42), channel_id=1, source_target_pairs={{0,4},{1,5},{2,6},{3,7},{4,8},{5,9},{6,10},{7,11},{8,12},{9,13},{1... | collective-permute-start | bytes 1720328 | tf_op jit(solution)/shard_map/ppermute | solution.py:21
  67.0 3.7 %copy-start.1 = (bf16[1,32,1792]{2,1,0:T(8,128)(2,1)S(1)}, bf16[1,32,1792]{2,1,0:T(8,128)(2,1)}, u32[]{:S(2)}) copy-start(bf16[1,32,1792]{2,1,0:T(8,128)(2,1)} %get-tuple-element.55) | copy-start | bytes 344068
  68.8 2.6 %collective-permute-start.7 = (f32[2,128]{1,0:T(2,128)S(1)}, f32[2,128]{1,0:T(2,128)S(1)}, u32[]{:S(2)}, u32[]{:S(2)}) collective-permute-start(f32[2,128]{1,0:T(2,128)S(1)} %pad_maximum_fusion.30), channel_id=1, source_target_pairs={{0,16},{1,17},{2,18},{3,19},{4,20},{5,21},{6,22},{7,23},{8,24},{9,... | collective-permute-start | bytes 3080 | tf_op jit(solution)/shard_map/ppermute | solution.py:33
  70.8 73.7 %collective-permute-start.6 = (bf16[128,7168]{1,0:T(8,128)(2,1)}, bf16[128,7168]{1,0:T(8,128)(2,1)S(1)}, u32[]{:S(2)}, u32[]{:S(2)}) collective-permute-start(bf16[128,7168]{1,0:T(8,128)(2,1)} %bitcast), channel_id=1, source_target_pairs={{0,16},{1,17},{2,18},{3,19},{4,20},{5,21},{6,22},{7,23},{8,24},{9,... | collective-permute-start | bytes 5505032 | tf_op jit(solution)/shard_map/ppermute | solution.py:33
  73.1 79.7 %all-to-all-start.1 = ((bf16[4,256,1792]{1,2,0:T(8,128)(2,1)}), bf16[4,256,1792]{1,2,0:T(8,128)(2,1)}, u32[]{:S(2)}, u32[]{:S(2)}) async-start(bf16[4,256,1792]{1,2,0:T(8,128)(2,1)} %bitcast.201), calls=%async_computation.1 | async-start | bytes 7340032 | tf_op jit(solution)/shard_map/all_to_all | solution.py:69
  77.9 2.8 %copy-start = (bf16[4,4,40,1792]{3,2,1,0:T(8,128)(2,1)S(1)}, bf16[4,4,40,1792]{3,2,1,0:T(8,128)(2,1)}, u32[]{:S(2)}) copy-start(bf16[4,4,40,1792]{3,2,1,0:T(8,128)(2,1)} %pad_maximum_fusion) | copy-start | bytes 6881284
  82.8 23.2 %collective-permute-start.9 = (bf16[4,32,1792]{2,1,0:T(8,128)(2,1)S(1)}, bf16[4,32,1792]{2,1,0:T(8,128)(2,1)S(1)}, u32[]{:S(2)}, u32[]{:S(2)}) collective-permute-start(bf16[4,32,1792]{2,1,0:T(8,128)(2,1)S(1)} %get-tuple-element.19), channel_id=1, source_target_pairs={{0,8},{1,9},{2,10},{3,11},{4,12},{5,13},{6,14},{7,15},{8,0},{9,1},... | collective-permute-start | bytes 1376264 | tf_op jit(solution)/shard_map/ppermute | solution.py:21
  85.8 20.1 %collective-permute-start.10 = (bf16[4,32,1792]{2,1,0:T(8,128)(2,1)S(1)}, bf16[4,32,1792]{2,1,0:T(8,128)(2,1)S(1)}, u32[]{:S(2)}, u32[]{:S(2)}) collective-permute-start(bf16[4,32,1792]{2,1,0:T(8,128)(2,1)S(1)} %get-tuple-element.45), channel_id=1, source_target_pairs={{0,12},{1,13},{2,14},{3,15},{4,0},{5,1},{6,2},{7,3},{8,4},{9,5},{1... | collective-permute-start | bytes 1376264 | tf_op jit(solution)/shard_map/ppermute | solution.py:21
  86.7 20.0 %collective-permute-start.8 = (bf16[4,32,1792]{2,1,0:T(8,128)(2,1)S(1)}, bf16[4,32,1792]{2,1,0:T(8,128)(2,1)S(1)}, u32[]{:S(2)}, u32[]{:S(2)}) collective-permute-start(bf16[4,32,1792]{2,1,0:T(8,128)(2,1)S(1)} %get-tuple-element.44), channel_id=1, source_target_pairs={{0,4},{1,5},{2,6},{3,7},{4,8},{5,9},{6,10},{7,11},{8,12},{9,13},{1... | collective-permute-start | bytes 1376264 | tf_op jit(solution)/shard_map/ppermute | solution.py:21
  110.7 26.7 %collective-permute-start.13 = (bf16[1152,256]{1,0:T(8,128)(2,1)S(1)}, bf16[1152,256]{1,0:T(8,128)(2,1)S(1)}, u32[]{:S(2)}, u32[]{:S(2)}) collective-permute-start(bf16[1152,256]{1,0:T(8,128)(2,1)S(1)} %pad_maximum_fusion.5), channel_id=1, source_target_pairs={{0,1},{1,2},{2,3},{3,0},{4,5},{5,6},{6,7},{7,4},{8,9},{9,10},{10,1... | collective-permute-start | bytes 1769480 | tf_op jit(solution)/shard_map/ppermute | solution.py:21
  113.7 29.8 %collective-permute-start.12 = (bf16[1152,256]{1,0:T(8,128)(2,1)S(1)}, bf16[1152,256]{1,0:T(8,128)(2,1)S(1)}, u32[]{:S(2)}, u32[]{:S(2)}) collective-permute-start(bf16[1152,256]{1,0:T(8,128)(2,1)S(1)} %pad_maximum_fusion.4), channel_id=1, source_target_pairs={{0,2},{1,3},{2,0},{3,1},{4,6},{5,7},{6,4},{7,5},{8,10},{9,11},{10,... | collective-permute-start | bytes 1769480 | tf_op jit(solution)/shard_map/ppermute | solution.py:21
  116.4 27.9 %collective-permute-start.11 = (bf16[1152,256]{1,0:T(8,128)(2,1)S(1)}, bf16[1152,256]{1,0:T(8,128)(2,1)S(1)}, u32[]{:S(2)}, u32[]{:S(2)}) collective-permute-start(bf16[1152,256]{1,0:T(8,128)(2,1)S(1)} %pad_maximum_fusion.3), channel_id=1, source_target_pairs={{0,3},{1,0},{2,1},{3,2},{4,7},{5,4},{6,5},{7,6},{8,11},{9,8},{10,9... | collective-permute-start | bytes 1769480 | tf_op jit(solution)/shard_map/ppermute | solution.py:21
  145.7 9.1 %collective-permute-start.15 = (bf16[640,256]{1,0:T(8,128)(2,1)}, bf16[640,256]{1,0:T(8,128)(2,1)S(1)}, u32[]{:S(2)}, u32[]{:S(2)}) collective-permute-start(bf16[640,256]{1,0:T(8,128)(2,1)} %bitcast.53), channel_id=1, source_target_pairs={{0,2},{1,3},{2,0},{3,1},{4,6},{5,7},{6,4},{7,5},{8,10},{9,11},{10,... | collective-permute-start | bytes 983048 | tf_op jit(solution)/shard_map/ppermute | solution.py:21
  149.4 14.2 %collective-permute-start.14 = (bf16[640,256]{1,0:T(8,128)(2,1)}, bf16[640,256]{1,0:T(8,128)(2,1)S(1)}, u32[]{:S(2)}, u32[]{:S(2)}) collective-permute-start(bf16[640,256]{1,0:T(8,128)(2,1)} %bitcast.51), channel_id=1, source_target_pairs={{0,1},{1,2},{2,3},{3,0},{4,5},{5,6},{6,7},{7,4},{8,9},{9,10},{10,1... | collective-permute-start | bytes 983048 | tf_op jit(solution)/shard_map/ppermute | solution.py:21
  151.3 13.1 %collective-permute-start.16 = (bf16[640,256]{1,0:T(8,128)(2,1)}, bf16[640,256]{1,0:T(8,128)(2,1)}, u32[]{:S(2)}, u32[]{:S(2)}) collective-permute-start(bf16[640,256]{1,0:T(8,128)(2,1)} %bitcast.55), channel_id=1, source_target_pairs={{0,3},{1,0},{2,1},{3,2},{4,7},{5,4},{6,5},{7,6},{8,11},{9,8},{10,9... | collective-permute-start | bytes 983048 | tf_op jit(solution)/shard_map/ppermute | solution.py:21
  171.9 38.6 %collective-permute-start.18 = (bf16[4,40,1792]{2,1,0:T(8,128)(2,1)}, bf16[4,40,1792]{2,1,0:T(8,128)(2,1)}, u32[]{:S(2)}, u32[]{:S(2)}) collective-permute-start(bf16[4,40,1792]{2,1,0:T(8,128)(2,1)} %bitcast.59), channel_id=1, source_target_pairs={{0,4},{1,5},{2,6},{3,7},{4,8},{5,9},{6,10},{7,11},{8,12},{9,13},{1... | collective-permute-start | bytes 1720328 | tf_op jit(solution)/shard_map/ppermute | solution.py:21
  182.9 27.6 %collective-permute-start.17 = (bf16[4,40,1792]{2,1,0:T(8,128)(2,1)}, bf16[4,40,1792]{2,1,0:T(8,128)(2,1)}, u32[]{:S(2)}, u32[]{:S(2)}) collective-permute-start(bf16[4,40,1792]{2,1,0:T(8,128)(2,1)} %bitcast.58), channel_id=1, source_target_pairs={{0,12},{1,13},{2,14},{3,15},{4,0},{5,1},{6,2},{7,3},{8,4},{9,5},{1... | collective-permute-start | bytes 1720328 | tf_op jit(solution)/shard_map/ppermute | solution.py:21
  184.4 26.1 %collective-permute-start.19 = (bf16[4,40,1792]{2,1,0:T(8,128)(2,1)S(1)}, bf16[4,40,1792]{2,1,0:T(8,128)(2,1)}, u32[]{:S(2)}, u32[]{:S(2)}) collective-permute-start(bf16[4,40,1792]{2,1,0:T(8,128)(2,1)S(1)} %bitcast.226), channel_id=1, source_target_pairs={{0,8},{1,9},{2,10},{3,11},{4,12},{5,13},{6,14},{7,15},{8,0},{9,1},... | collective-permute-start | bytes 1720328 | tf_op jit(solution)/shard_map/ppermute | solution.py:21
  186.0 7.2 %collective-permute-start.25 = (bf16[512,256]{1,0:T(8,128)(2,1)S(1)}, bf16[512,256]{1,0:T(8,128)(2,1)S(1)}, u32[]{:S(2)}, u32[]{:S(2)}) collective-permute-start(bf16[512,256]{1,0:T(8,128)(2,1)S(1)} %bitcast.244), channel_id=1, source_target_pairs={{0,2},{1,3},{2,0},{3,1},{4,6},{5,7},{6,4},{7,5},{8,10},{9,11},{10,... | collective-permute-start | bytes 786440 | tf_op jit(solution)/shard_map/ppermute | solution.py:21
  188.7 11.8 %collective-permute-start.24 = (bf16[512,256]{1,0:T(8,128)(2,1)S(1)}, bf16[512,256]{1,0:T(8,128)(2,1)S(1)}, u32[]{:S(2)}, u32[]{:S(2)}) collective-permute-start(bf16[512,256]{1,0:T(8,128)(2,1)S(1)} %bitcast.242), channel_id=1, source_target_pairs={{0,1},{1,2},{2,3},{3,0},{4,5},{5,6},{6,7},{7,4},{8,9},{9,10},{10,1... | collective-permute-start | bytes 786440 | tf_op jit(solution)/shard_map/ppermute | solution.py:21
  193.2 9.2 %collective-permute-start.26 = (bf16[512,256]{1,0:T(8,128)(2,1)S(1)}, bf16[512,256]{1,0:T(8,128)(2,1)S(1)}, u32[]{:S(2)}, u32[]{:S(2)}) collective-permute-start(bf16[512,256]{1,0:T(8,128)(2,1)S(1)} %bitcast.243), channel_id=1, source_target_pairs={{0,3},{1,0},{2,1},{3,2},{4,7},{5,4},{6,5},{7,6},{8,11},{9,8},{10,9... | collective-permute-start | bytes 786440 | tf_op jit(solution)/shard_map/ppermute | solution.py:21
  206.1 29.7 %all-to-all-start.2 = ((bf16[4,4,32,1792]{3,2,1,0:T(8,128)(2,1)}), bf16[4,4,32,1792]{3,2,1,0:T(8,128)(2,1)}, u32[]{:S(2)}, u32[]{:S(2)}) async-start(bf16[4,4,32,1792]{3,2,1,0:T(8,128)(2,1)} %pad_maximum_fusion.2), calls=%async_computation.2 | async-start | bytes 3670016 | tf_op jit(solution)/shard_map/all_to_all | solution.py:69
  212.4 9.4 %collective-permute-start.20 = (bf16[80,1792]{1,0:T(8,128)(2,1)S(1)}, bf16[80,1792]{1,0:T(8,128)(2,1)S(1)}, u32[]{:S(2)}, u32[]{:S(2)}) collective-permute-start(bf16[80,1792]{1,0:T(8,128)(2,1)S(1)} %pad_maximum_fusion.16), channel_id=1, source_target_pairs={{0,16},{1,17},{2,18},{3,19},{4,20},{5,21},{6,22},{7,23},{8,24},{9,... | collective-permute-start | bytes 860168 | tf_op jit(solution)/shard_map/ppermute | solution.py:33
  216.5 6.7 %collective-permute-start.21 = (bf16[80,1792]{1,0:T(8,128)(2,1)S(1)}, bf16[80,1792]{1,0:T(8,128)(2,1)S(1)}, u32[]{:S(2)}, u32[]{:S(2)}) collective-permute-start(bf16[80,1792]{1,0:T(8,128)(2,1)S(1)} %pad_maximum_fusion.17), channel_id=1, source_target_pairs={{0,19},{1,16},{2,17},{3,18},{4,23},{5,20},{6,21},{7,22},{8,27},{9,... | collective-permute-start | bytes 860168 | tf_op jit(solution)/shard_map/ppermute | solution.py:33
  218.5 7.9 %collective-permute-start.22 = (bf16[80,1792]{1,0:T(8,128)(2,1)S(1)}, bf16[80,1792]{1,0:T(8,128)(2,1)S(1)}, u32[]{:S(2)}, u32[]{:S(2)}) collective-permute-start(bf16[80,1792]{1,0:T(8,128)(2,1)S(1)} %pad_maximum_fusion.18), channel_id=1, source_target_pairs={{0,18},{1,19},{2,16},{3,17},{4,22},{5,23},{6,20},{7,21},{8,26},{9,... | collective-permute-start | bytes 860168 | tf_op jit(solution)/shard_map/ppermute | solution.py:33
  221.7 13.8 %collective-permute-start.23 = (bf16[80,1792]{1,0:T(8,128)(2,1)S(1)}, bf16[80,1792]{1,0:T(8,128)(2,1)S(1)}, u32[]{:S(2)}, u32[]{:S(2)}) collective-permute-start(bf16[80,1792]{1,0:T(8,128)(2,1)S(1)} %pad_maximum_fusion.19), channel_id=1, source_target_pairs={{0,17},{1,18},{2,19},{3,16},{4,21},{5,22},{6,23},{7,20},{8,25},{9,... | collective-permute-start | bytes 860168 | tf_op jit(solution)/shard_map/ppermute | solution.py:33
  238.0 6.9 %collective-permute-start.27 = (bf16[64,1792]{1,0:T(8,128)(2,1)S(1)}, bf16[64,1792]{1,0:T(8,128)(2,1)S(1)}, u32[]{:S(2)}, u32[]{:S(2)}) collective-permute-start(bf16[64,1792]{1,0:T(8,128)(2,1)S(1)} %pad_maximum_fusion.26), channel_id=1, source_target_pairs={{0,16},{1,17},{2,18},{3,19},{4,20},{5,21},{6,22},{7,23},{8,24},{9,... | collective-permute-start | bytes 688136 | tf_op jit(solution)/shard_map/ppermute | solution.py:33
  238.8 8.1 %collective-permute-start.28 = (bf16[64,1792]{1,0:T(8,128)(2,1)S(1)}, bf16[64,1792]{1,0:T(8,128)(2,1)S(1)}, u32[]{:S(2)}, u32[]{:S(2)}) collective-permute-start(bf16[64,1792]{1,0:T(8,128)(2,1)S(1)} %pad_maximum_fusion.27), channel_id=1, source_target_pairs={{0,19},{1,16},{2,17},{3,18},{4,23},{5,20},{6,21},{7,22},{8,27},{9,... | collective-permute-start | bytes 688136 | tf_op jit(solution)/shard_map/ppermute | solution.py:33
  240.5 7.0 %collective-permute-start.29 = (bf16[64,1792]{1,0:T(8,128)(2,1)S(1)}, bf16[64,1792]{1,0:T(8,128)(2,1)S(1)}, u32[]{:S(2)}, u32[]{:S(2)}) collective-permute-start(bf16[64,1792]{1,0:T(8,128)(2,1)S(1)} %pad_maximum_fusion.28), channel_id=1, source_target_pairs={{0,18},{1,19},{2,16},{3,17},{4,22},{5,23},{6,20},{7,21},{8,26},{9,... | collective-permute-start | bytes 688136 | tf_op jit(solution)/shard_map/ppermute | solution.py:33
  243.3 11.7 %collective-permute-start.30 = (bf16[64,1792]{1,0:T(8,128)(2,1)S(1)}, bf16[64,1792]{1,0:T(8,128)(2,1)S(1)}, u32[]{:S(2)}, u32[]{:S(2)}) collective-permute-start(bf16[64,1792]{1,0:T(8,128)(2,1)S(1)} %pad_maximum_fusion.29), channel_id=1, source_target_pairs={{0,17},{1,18},{2,19},{3,16},{4,21},{5,22},{6,23},{7,20},{8,25},{9,... | collective-permute-start | bytes 688136 | tf_op jit(solution)/shard_map/ppermute | solution.py:33

commit v3 on v2

--- a/solution.py
+++ b/solution.py
@@ -160,12 +160,12 @@
             ours = (back[0] + jnp.where(even, back[1], back[3])).astype(jnp.bfloat16)
             theirs = (back[2] + jnp.where(even, back[3], back[1])).astype(jnp.bfloat16)
         messages = [jnp.concatenate([ours[step], theirs[step]]) for step in range(SIDE)]
-        if c:
-            messages = [tie(message, *landed) for message in messages]
-        landed = [shift_on(message, -step) for step, message in enumerate(messages)]
+        landed.append([shift_on(message, -step) for step, message in enumerate(messages)])
+    for c in cuts:
         chosen = table[:, starts[c] : starts[c] + EXPERTS * CUTS[c]]
         for step in range(SIDE):
-            combined = jnp.dot(chosen, landed[step], preferred_element_type=jnp.float32)
+            arrived = landed[c][step] if c else tie(landed[c][step], *messages)
+            combined = jnp.dot(chosen, arrived, preferred_element_type=jnp.float32)
             part = lax.dynamic_slice(result, (0, quarter(step)), (count, PART))
             updated = part.astype(jnp.float32) + facts_before[1][:, None] * combined
             result = lax.dynamic_update_slice(result, updated.astype(jnp.bfloat16), (0, quarter(step)))

time: 261 us -> 260 us (level)
  waiting for transfers between devices: 113 us -> 104 us
  other arithmetic: 14 us -> 17.5 us
    ppermute x10, waiting for transfers between devices: 22.5 us -> 7.71 us  [shift_on(): return lax.ppermute(block, ('pipe', 'expert'), pairs)]
    all_to_all x3, waiting for transfers between devices: 1.7 us -> 8.87 us  [exchange(): lax.all_to_all(pieces, 'expert', 0, 0, axis_index_groups=groups, tiled=True)]
    ppermute x10, starting transfers between devices: 18.1 us -> 22.5 us  [shift_on(): return lax.ppermute(block, ('pipe', 'expert'), pairs)]
    ppermute x21, starting transfers between devices: 45.6 us -> 41.9 us  [shift(): return lax.ppermute(block, 'expert', pairs)]
    concatenate x8, other arithmetic: 0.15 us -> 3.02 us  [per_device(): jnp.concatenate([ours[step], theirs[step]])]
    unnamed x11 -> x9, local copies, waits for them, and re-layouts: 7.65 us -> 7.62 us
  transfers between devices with their start and end apart: 34 -> 34, of which waited for: 20 -> 18; matrix products, arithmetic and copies ran while one was open for 20% -> 22% of each run, Pallas kernels for 0% -> 0%
where the time goes in v3:
time: 260 us; the launch traced here: 255 us
  waiting for transfers between devices  104 us (40%)
  starting transfers between devices  78.4 us (30%)
  matrix products  42.5 us (16%)
  other arithmetic  17.5 us (7%)
  local copies, waits for them, and re-layouts  10.8 us (4%)
    ppermute x21, waiting for transfers between devices, shift(): return lax.ppermute(block, 'expert', pairs)  87.8 us
    ppermute x21, starting transfers between devices, shift(): return lax.ppermute(block, 'expert', pairs)  41.9 us
    ppermute x10, starting transfers between devices, shift_on(): return lax.ppermute(block, ('pipe', 'expert'), pairs)  22.5 us
    dot_general x8, matrix products, per_device(): jnp.dot(received[c], of(ups, -step), preferred_element_type=jnp.float32)  15.9 us
    dot_general x8, matrix products, per_device(): jnp.dot(gathered[c][step], of(downs, -step), preferred_element_type=jnp.f...  15.7 us
    all_to_all x3, starting transfers between devices, exchange(): lax.all_to_all(pieces, 'expert', 0, 0, axis_index_groups=groups, tiled=True)  14 us
    all_to_all x3, waiting for transfers between devices, exchange(): lax.all_to_all(pieces, 'expert', 0, 0, axis_index_groups=groups, tiled=True)  8.87 us
    ppermute x10, waiting for transfers between devices, shift_on(): return lax.ppermute(block, ('pipe', 'expert'), pairs)  7.71 us
  transfers between devices with their start and end apart: 34, of which 18 were waited for; matrix products, arithmetic and copies ran while one was open for 22% of the time, Pallas kernels for 0%

profile of v3, /device:TPU:1, one launch (start us, length us, event | category | flops | bytes accessed | tf_op | source)
XLA Modules:
  0.0 254.6 jit_solution(16705702373381218843)
XLA Ops:
  1.1 2.0 multiply_reduce_fusion
  4.6 2.1 collective-permute-start
  8.1 2.5 collective-permute-start.1
  10.7 2.2 convolution_convert_fusion
  14.0 4.9 %all-to-all-start = ((bf16[4,1792,256]{2,1,0:T(8,128)(2,1)}), bf16[4,1792,256]{2,1,0:T(8,128)(2,1)}, u32[]{:S(2)}, u32[]{:S(2)}) async-start(bf16[4,1792,256]{2,1,0:T(8,128)(2,1)} %bitcast.210), calls=%async_computation | async-start | bytes 7340032 | tf_op jit(solution)/shard_map/all_to_all | solution.py:69
  22.4 5.8 %copy.6 = bf16[1,256,7168]{1,2,0:T(8,128)(2,1)} copy(bf16[1,256,7168]{2,1,0:T(8,128)(2,1)} %param.7) | data formatting | bytes 7340032 | tf_op args[2]
  28.3 3.1 %collective-permute-done.1 = bf16[144,1792]{1,0:T(8,128)(2,1)S(1)} collective-permute-done((bf16[144,1792]{1,0:T(8,128)(2,1)S(1)}, bf16[144,1792]{1,0:T(8,128)(2,1)S(1)}, u32[]{:S(2)}, u32[]{:S(2)}) %collective-permute-start.1) | collective-permute-done | bytes 516128 | tf_op jit(solution)/shard_map/ppermute | solution.py:21
  32.5 3.2 %collective-permute-start.4 = (bf16[4,40,1792]{2,1,0:T(8,128)(2,1)S(1)}, bf16[4,40,1792]{2,1,0:T(8,128)(2,1)S(1)}, u32[]{:S(2)}, u32[]{:S(2)}) collective-permute-start(bf16[4,40,1792]{2,1,0:T(8,128)(2,1)S(1)} %pad_maximum_fusion.7), channel_id=1, source_target_pairs={{0,8},{1,9},{2,10},{3,11},{4,12},{5,13},{6,14},{7,15},{8,0},{9,1},... | collective-permute-start | bytes 1720328 | tf_op jit(solution)/shard_map/ppermute | solution.py:21
  36.4 2.3 collective-permute-start.5
  38.8 6.4 %collective-permute-done.4 = bf16[4,40,1792]{2,1,0:T(8,128)(2,1)S(1)} collective-permute-done((bf16[4,40,1792]{2,1,0:T(8,128)(2,1)S(1)}, bf16[4,40,1792]{2,1,0:T(8,128)(2,1)S(1)}, u32[]{:S(2)}, u32[]{:S(2)}) %collective-permute-start.4) | collective-permute-done | bytes 573472 | tf_op jit(solution)/shard_map/ppermute | solution.py:21
  45.1 16.4 %collective-permute-done.3 = bf16[4,40,1792]{2,1,0:T(8,128)(2,1)S(1)} collective-permute-done((bf16[4,40,1792]{2,1,0:T(8,128)(2,1)S(1)}, bf16[4,40,1792]{2,1,0:T(8,128)(2,1)S(1)}, u32[]{:S(2)}, u32[]{:S(2)}) %collective-permute-start.3) | collective-permute-done | bytes 573472 | tf_op jit(solution)/shard_map/ppermute | solution.py:21
  63.3 2.3 collective-permute-start.7
  66.4 4.5 %all-to-all-done = bf16[4,1792,256]{2,1,0:T(8,128)(2,1)} async-done(((bf16[4,1792,256]{2,1,0:T(8,128)(2,1)}), bf16[4,1792,256]{2,1,0:T(8,128)(2,1)}, u32[]{:S(2)}, u32[]{:S(2)}) %all-to-all-start) | async-done | bytes 3670048 | tf_op jit(solution)/shard_map/all_to_all | solution.py:69
  70.9 4.8 %all-to-all-start.1 = ((bf16[4,256,1792]{1,2,0:T(8,128)(2,1)}), bf16[4,256,1792]{1,2,0:T(8,128)(2,1)}, u32[]{:S(2)}, u32[]{:S(2)}) async-start(bf16[4,256,1792]{1,2,0:T(8,128)(2,1)} %bitcast.201), calls=%async_computation.1 | async-start | bytes 7340032 | tf_op jit(solution)/shard_map/all_to_all | solution.py:69
  75.6 2.8 %convolution_convert_fusion.6 = bf16[640,256]{1,0:T(8,128)(2,1)S(1)} fusion(bf16[640,1792]{1,0:T(8,128)(2,1)} %bitcast.212, bf16[4,1792,256]{2,1,0:T(8,128)(2,1)} %all-to-all-done, s32[]{:T(128)S(6)} %select_n.290), kind=kOutput, calls=%fused_computation.34 | convolution fusion | flops 587366400 | bytes 3538948 | tf_op jit(solution)/shard_map/dot_general | solution.py:126
  78.5 1.9 convolution_convert_fusion.4
  80.5 3.0 %collective-permute-start.9 = (bf16[4,32,1792]{2,1,0:T(8,128)(2,1)S(1)}, bf16[4,32,1792]{2,1,0:T(8,128)(2,1)S(1)}, u32[]{:S(2)}, u32[]{:S(2)}) collective-permute-start(bf16[4,32,1792]{2,1,0:T(8,128)(2,1)S(1)} %get-tuple-element.19), channel_id=1, source_target_pairs={{0,8},{1,9},{2,10},{3,11},{4,12},{5,13},{6,14},{7,15},{8,0},{9,1},... | collective-permute-start | bytes 1376264 | tf_op jit(solution)/shard_map/ppermute | solution.py:21
  84.0 2.5 collective-permute-start.10
  86.6 1.9 convolution_convert_fusion.5
  88.6 15.8 %collective-permute-done.8 = bf16[4,32,1792]{2,1,0:T(8,128)(2,1)S(1)} collective-permute-done((bf16[4,32,1792]{2,1,0:T(8,128)(2,1)S(1)}, bf16[4,32,1792]{2,1,0:T(8,128)(2,1)S(1)}, u32[]{:S(2)}, u32[]{:S(2)}) %collective-permute-start.8) | collective-permute-done | bytes 458784 | tf_op jit(solution)/shard_map/ppermute | solution.py:21
  106.6 1.8 convolution_convert_fusion.7
  108.5 3.1 %collective-permute-start.11 = (bf16[1152,256]{1,0:T(8,128)(2,1)S(1)}, bf16[1152,256]{1,0:T(8,128)(2,1)S(1)}, u32[]{:S(2)}, u32[]{:S(2)}) collective-permute-start(bf16[1152,256]{1,0:T(8,128)(2,1)S(1)} %pad_maximum_fusion.3), channel_id=1, source_target_pairs={{0,3},{1,0},{2,1},{3,2},{4,7},{5,4},{6,5},{7,6},{8,11},{9,8},{10,9... | collective-permute-start | bytes 1769480 | tf_op jit(solution)/shard_map/ppermute | solution.py:21
  115.4 1.9 fusion.47
  117.3 1.8 fusion.45
  119.2 13.0 %collective-permute-done.11 = bf16[1152,256]{1,0:T(8,128)(2,1)S(1)} collective-permute-done((bf16[1152,256]{1,0:T(8,128)(2,1)S(1)}, bf16[1152,256]{1,0:T(8,128)(2,1)S(1)}, u32[]{:S(2)}, u32[]{:S(2)}) %collective-permute-start.11) | collective-permute-done | bytes 589856 | tf_op jit(solution)/shard_map/ppermute | solution.py:21
  132.2 12.3 %collective-permute-done.13 = bf16[1152,256]{1,0:T(8,128)(2,1)S(1)} collective-permute-done((bf16[1152,256]{1,0:T(8,128)(2,1)S(1)}, bf16[1152,256]{1,0:T(8,128)(2,1)S(1)}, u32[]{:S(2)}, u32[]{:S(2)}) %collective-permute-start.13) | collective-permute-done | bytes 589856 | tf_op jit(solution)/shard_map/ppermute | solution.py:21
  149.3 2.0 fusion.37
  151.3 3.8 %collective-permute-done.16 = bf16[640,256]{1,0:T(8,128)(2,1)} collective-permute-done((bf16[640,256]{1,0:T(8,128)(2,1)}, bf16[640,256]{1,0:T(8,128)(2,1)}, u32[]{:S(2)}, u32[]{:S(2)}) %collective-permute-start.16) | collective-permute-done | bytes 327712 | tf_op jit(solution)/shard_map/ppermute | solution.py:21
  155.9 5.4 %collective-permute-done.15 = bf16[640,256]{1,0:T(8,128)(2,1)S(1)} collective-permute-done((bf16[640,256]{1,0:T(8,128)(2,1)}, bf16[640,256]{1,0:T(8,128)(2,1)S(1)}, u32[]{:S(2)}, u32[]{:S(2)}) %collective-permute-start.15) | collective-permute-done | bytes 327712 | tf_op jit(solution)/shard_map/ppermute | solution.py:21
  161.4 2.0 fusion.33
  163.4 2.0 fusion.29
  165.3 2.3 add_convert_fusion
  168.8 12.8 %collective-permute-start.17 = (bf16[4,40,1792]{2,1,0:T(8,128)(2,1)}, bf16[4,40,1792]{2,1,0:T(8,128)(2,1)}, u32[]{:S(2)}, u32[]{:S(2)}) collective-permute-start(bf16[4,40,1792]{2,1,0:T(8,128)(2,1)} %bitcast.58), channel_id=1, source_target_pairs={{0,12},{1,13},{2,14},{3,15},{4,0},{5,1},{6,2},{7,3},{8,4},{9,5},{1... | collective-permute-start | bytes 1720328 | tf_op jit(solution)/shard_map/ppermute | solution.py:21
  183.3 3.1 %collective-permute-start.23 = (bf16[512,256]{1,0:T(8,128)(2,1)S(1)}, bf16[512,256]{1,0:T(8,128)(2,1)S(1)}, u32[]{:S(2)}, u32[]{:S(2)}) collective-permute-start(bf16[512,256]{1,0:T(8,128)(2,1)S(1)} %bitcast.242), channel_id=1, source_target_pairs={{0,3},{1,0},{2,1},{3,2},{4,7},{5,4},{6,5},{7,6},{8,11},{9,8},{10,9... | collective-permute-start | bytes 786440 | tf_op jit(solution)/shard_map/ppermute | solution.py:21
  186.6 1.9 fusion.35
  188.4 4.9 %collective-permute-done.21 = bf16[512,256]{1,0:T(8,128)(2,1)S(1)} collective-permute-done((bf16[512,256]{1,0:T(8,128)(2,1)S(1)}, bf16[512,256]{1,0:T(8,128)(2,1)S(1)}, u32[]{:S(2)}, u32[]{:S(2)}) %collective-permute-start.21) | collective-permute-done | bytes 262176 | tf_op jit(solution)/shard_map/ppermute | solution.py:21
  193.4 1.9 fusion.31
  195.2 4.9 %collective-permute-done.22 = bf16[512,256]{1,0:T(8,128)(2,1)S(1)} collective-permute-done((bf16[512,256]{1,0:T(8,128)(2,1)S(1)}, bf16[512,256]{1,0:T(8,128)(2,1)S(1)}, u32[]{:S(2)}, u32[]{:S(2)}) %collective-permute-start.22) | collective-permute-done | bytes 262176 | tf_op jit(solution)/shard_map/ppermute | solution.py:21
  200.1 1.9 fusion.27
  202.0 1.9 add_convert_fusion.1
  205.5 4.4 %all-to-all-start.2 = ((bf16[4,4,32,1792]{3,2,1,0:T(8,128)(2,1)}), bf16[4,4,32,1792]{3,2,1,0:T(8,128)(2,1)}, u32[]{:S(2)}, u32[]{:S(2)}) async-start(bf16[4,4,32,1792]{3,2,1,0:T(8,128)(2,1)} %pad_maximum_fusion.2), calls=%async_computation.2 | async-start | bytes 3670016 | tf_op jit(solution)/shard_map/all_to_all | solution.py:69
  212.6 5.5 %collective-permute-start.26 = (bf16[80,1792]{1,0:T(8,128)(2,1)}, bf16[80,1792]{1,0:T(8,128)(2,1)S(1)}, u32[]{:S(2)}, u32[]{:S(2)}) collective-permute-start(bf16[80,1792]{1,0:T(8,128)(2,1)} %pad_maximum_fusion.19), channel_id=1, source_target_pairs={{0,17},{1,18},{2,19},{3,16},{4,21},{5,22},{6,23},{7,20},{8,25},{9,... | collective-permute-start | bytes 860168 | tf_op jit(solution)/shard_map/ppermute | solution.py:33
  219.8 3.6 %collective-permute-start.24 = (bf16[80,1792]{1,0:T(8,128)(2,1)}, bf16[80,1792]{1,0:T(8,128)(2,1)}, u32[]{:S(2)}, u32[]{:S(2)}) collective-permute-start(bf16[80,1792]{1,0:T(8,128)(2,1)} %pad_maximum_fusion.17), channel_id=1, source_target_pairs={{0,19},{1,16},{2,17},{3,18},{4,23},{5,20},{6,21},{7,22},{8,27},{9,... | collective-permute-start | bytes 860168 | tf_op jit(solution)/shard_map/ppermute | solution.py:33
  224.9 4.4 %all-to-all-done.2 = bf16[4,4,32,1792]{3,2,1,0:T(8,128)(2,1)} async-done(((bf16[4,4,32,1792]{3,2,1,0:T(8,128)(2,1)}), bf16[4,4,32,1792]{3,2,1,0:T(8,128)(2,1)}, u32[]{:S(2)}, u32[]{:S(2)}) %all-to-all-start.2) | async-done | bytes 1835040 | tf_op jit(solution)/shard_map/all_to_all | solution.py:69
  229.3 1.9 convert_element_type.253
  231.5 6.7 %collective-permute-start.27 = (bf16[64,1792]{1,0:T(8,128)(2,1)S(1)}, bf16[64,1792]{1,0:T(8,128)(2,1)S(1)}, u32[]{:S(2)}, u32[]{:S(2)}) collective-permute-start(bf16[64,1792]{1,0:T(8,128)(2,1)S(1)} %pad_maximum_fusion.26), channel_id=1, source_target_pairs={{0,16},{1,17},{2,18},{3,19},{4,20},{5,21},{6,22},{7,23},{8,24},{9,... | collective-permute-start | bytes 688136 | tf_op jit(solution)/shard_map/ppermute | solution.py:33
  238.4 2.6 %collective-permute-start.29 = (bf16[64,1792]{1,0:T(8,128)(2,1)S(1)}, bf16[64,1792]{1,0:T(8,128)(2,1)S(1)}, u32[]{:S(2)}, u32[]{:S(2)}) collective-permute-start(bf16[64,1792]{1,0:T(8,128)(2,1)S(1)} %pad_maximum_fusion.28), channel_id=1, source_target_pairs={{0,18},{1,19},{2,16},{3,17},{4,22},{5,23},{6,20},{7,21},{8,26},{9,... | collective-permute-start | bytes 688136 | tf_op jit(solution)/shard_map/ppermute | solution.py:33
  245.0 4.0 %collective-permute-done.28 = bf16[64,1792]{1,0:T(8,128)(2,1)S(1)} collective-permute-done((bf16[64,1792]{1,0:T(8,128)(2,1)S(1)}, bf16[64,1792]{1,0:T(8,128)(2,1)S(1)}, u32[]{:S(2)}, u32[]{:S(2)}) %collective-permute-start.28) | collective-permute-done | bytes 229408 | tf_op jit(solution)/shard_map/ppermute | solution.py:33
  (142 shorter events, 45.3 us)
Async XLA Ops:
  4.6 23.7 %collective-permute-start = (bf16[144,1792]{1,0:T(8,128)(2,1)S(1)}, bf16[144,1792]{1,0:T(8,128)(2,1)S(1)}, u32[]{:S(2)}, u32[]{:S(2)}) collective-permute-start(bf16[144,1792]{1,0:T(8,128)(2,1)S(1)} %convolution_convert_fusion.2), channel_id=1, source_target_pairs={{0,1},{1,2},{2,3},{3,0},{4,5},{5,6},{6,7},{7,4},{8,9},{9,10},{10,1... | collective-permute-start | bytes 1548296 | tf_op jit(solution)/shard_map/ppermute | solution.py:21
  8.1 23.3 %collective-permute-start.1 = (bf16[144,1792]{1,0:T(8,128)(2,1)S(1)}, bf16[144,1792]{1,0:T(8,128)(2,1)S(1)}, u32[]{:S(2)}, u32[]{:S(2)}) collective-permute-start(bf16[144,1792]{1,0:T(8,128)(2,1)S(1)} %convolution_convert_fusion.1), channel_id=1, source_target_pairs={{0,2},{1,3},{2,0},{3,1},{4,6},{5,7},{6,4},{7,5},{8,10},{9,11},{10,... | collective-permute-start | bytes 1548296 | tf_op jit(solution)/shard_map/ppermute | solution.py:21
  12.8 19.6 %collective-permute-start.2 = (bf16[144,1792]{1,0:T(8,128)(2,1)}, bf16[144,1792]{1,0:T(8,128)(2,1)S(1)}, u32[]{:S(2)}, u32[]{:S(2)}) collective-permute-start(bf16[144,1792]{1,0:T(8,128)(2,1)} %convolution_convert_fusion), channel_id=1, source_target_pairs={{0,3},{1,0},{2,1},{3,2},{4,7},{5,4},{6,5},{7,6},{8,11},{9,8},{10,9... | collective-permute-start | bytes 1548296 | tf_op jit(solution)/shard_map/ppermute | solution.py:21
  14.0 7.0 %copy-start.2 = (f32[4,1,32]{2,1,0:T(1,128)S(1)}, f32[4,1,32]{2,1,0:T(1,128)}, u32[]{:S(2)}) copy-start(f32[4,1,32]{2,1,0:T(1,128)} %param.9) | copy-start | bytes 1540
  14.0 56.9 %all-to-all-start = ((bf16[4,1792,256]{2,1,0:T(8,128)(2,1)}), bf16[4,1792,256]{2,1,0:T(8,128)(2,1)}, u32[]{:S(2)}, u32[]{:S(2)}) async-start(bf16[4,1792,256]{2,1,0:T(8,128)(2,1)} %bitcast.210), calls=%async_computation | async-start | bytes 7340032 | tf_op jit(solution)/shard_map/all_to_all | solution.py:69
  32.5 12.6 %collective-permute-start.4 = (bf16[4,40,1792]{2,1,0:T(8,128)(2,1)S(1)}, bf16[4,40,1792]{2,1,0:T(8,128)(2,1)S(1)}, u32[]{:S(2)}, u32[]{:S(2)}) collective-permute-start(bf16[4,40,1792]{2,1,0:T(8,128)(2,1)S(1)} %pad_maximum_fusion.7), channel_id=1, source_target_pairs={{0,8},{1,9},{2,10},{3,11},{4,12},{5,13},{6,14},{7,15},{8,0},{9,1},... | collective-permute-start | bytes 1720328 | tf_op jit(solution)/shard_map/ppermute | solution.py:21
  35.9 25.7 %collective-permute-start.3 = (bf16[4,40,1792]{2,1,0:T(8,128)(2,1)S(1)}, bf16[4,40,1792]{2,1,0:T(8,128)(2,1)S(1)}, u32[]{:S(2)}, u32[]{:S(2)}) collective-permute-start(bf16[4,40,1792]{2,1,0:T(8,128)(2,1)S(1)} %get-tuple-element.42), channel_id=1, source_target_pairs={{0,4},{1,5},{2,6},{3,7},{4,8},{5,9},{6,10},{7,11},{8,12},{9,13},{1... | collective-permute-start | bytes 1720328 | tf_op jit(solution)/shard_map/ppermute | solution.py:21
  36.4 25.2 %collective-permute-start.5 = (bf16[4,40,1792]{2,1,0:T(8,128)(2,1)S(1)}, bf16[4,40,1792]{2,1,0:T(8,128)(2,1)S(1)}, u32[]{:S(2)}, u32[]{:S(2)}) collective-permute-start(bf16[4,40,1792]{2,1,0:T(8,128)(2,1)S(1)} %get-tuple-element.43), channel_id=1, source_target_pairs={{0,12},{1,13},{2,14},{3,15},{4,0},{5,1},{6,2},{7,3},{8,4},{9,5},{1... | collective-permute-start | bytes 1720328 | tf_op jit(solution)/shard_map/ppermute | solution.py:21
  61.5 4.1 %copy-start.1 = (bf16[1,32,1792]{2,1,0:T(8,128)(2,1)S(1)}, bf16[1,32,1792]{2,1,0:T(8,128)(2,1)}, u32[]{:S(2)}) copy-start(bf16[1,32,1792]{2,1,0:T(8,128)(2,1)} %get-tuple-element.55) | copy-start | bytes 344068
  63.3 3.1 %collective-permute-start.7 = (f32[2,128]{1,0:T(2,128)S(1)}, f32[2,128]{1,0:T(2,128)S(1)}, u32[]{:S(2)}, u32[]{:S(2)}) collective-permute-start(f32[2,128]{1,0:T(2,128)S(1)} %pad_maximum_fusion.30), channel_id=1, source_target_pairs={{0,16},{1,17},{2,18},{3,19},{4,20},{5,21},{6,22},{7,23},{8,24},{9,... | collective-permute-start | bytes 3080 | tf_op jit(solution)/shard_map/ppermute | solution.py:33
  65.8 79.0 %collective-permute-start.6 = (bf16[128,7168]{1,0:T(8,128)(2,1)}, bf16[128,7168]{1,0:T(8,128)(2,1)S(1)}, u32[]{:S(2)}, u32[]{:S(2)}) collective-permute-start(bf16[128,7168]{1,0:T(8,128)(2,1)} %bitcast), channel_id=1, source_target_pairs={{0,16},{1,17},{2,18},{3,19},{4,20},{5,21},{6,22},{7,23},{8,24},{9,... | collective-permute-start | bytes 5505032 | tf_op jit(solution)/shard_map/ppermute | solution.py:33
  70.9 78.5 %all-to-all-start.1 = ((bf16[4,256,1792]{1,2,0:T(8,128)(2,1)}), bf16[4,256,1792]{1,2,0:T(8,128)(2,1)}, u32[]{:S(2)}, u32[]{:S(2)}) async-start(bf16[4,256,1792]{1,2,0:T(8,128)(2,1)} %bitcast.201), calls=%async_computation.1 | async-start | bytes 7340032 | tf_op jit(solution)/shard_map/all_to_all | solution.py:69
  75.6 2.8 %copy-start = (bf16[4,4,40,1792]{3,2,1,0:T(8,128)(2,1)S(1)}, bf16[4,4,40,1792]{3,2,1,0:T(8,128)(2,1)}, u32[]{:S(2)}) copy-start(bf16[4,4,40,1792]{3,2,1,0:T(8,128)(2,1)} %pad_maximum_fusion) | copy-start | bytes 6881284
  80.5 24.0 %collective-permute-start.9 = (bf16[4,32,1792]{2,1,0:T(8,128)(2,1)S(1)}, bf16[4,32,1792]{2,1,0:T(8,128)(2,1)S(1)}, u32[]{:S(2)}, u32[]{:S(2)}) collective-permute-start(bf16[4,32,1792]{2,1,0:T(8,128)(2,1)S(1)} %get-tuple-element.19), channel_id=1, source_target_pairs={{0,8},{1,9},{2,10},{3,11},{4,12},{5,13},{6,14},{7,15},{8,0},{9,1},... | collective-permute-start | bytes 1376264 | tf_op jit(solution)/shard_map/ppermute | solution.py:21
  83.5 20.9 %collective-permute-start.8 = (bf16[4,32,1792]{2,1,0:T(8,128)(2,1)S(1)}, bf16[4,32,1792]{2,1,0:T(8,128)(2,1)S(1)}, u32[]{:S(2)}, u32[]{:S(2)}) collective-permute-start(bf16[4,32,1792]{2,1,0:T(8,128)(2,1)S(1)} %get-tuple-element.44), channel_id=1, source_target_pairs={{0,4},{1,5},{2,6},{3,7},{4,8},{5,9},{6,10},{7,11},{8,12},{9,13},{1... | collective-permute-start | bytes 1376264 | tf_op jit(solution)/shard_map/ppermute | solution.py:21
  84.0 20.4 %collective-permute-start.10 = (bf16[4,32,1792]{2,1,0:T(8,128)(2,1)S(1)}, bf16[4,32,1792]{2,1,0:T(8,128)(2,1)S(1)}, u32[]{:S(2)}, u32[]{:S(2)}) collective-permute-start(bf16[4,32,1792]{2,1,0:T(8,128)(2,1)S(1)} %get-tuple-element.45), channel_id=1, source_target_pairs={{0,12},{1,13},{2,14},{3,15},{4,0},{5,1},{6,2},{7,3},{8,4},{9,5},{1... | collective-permute-start | bytes 1376264 | tf_op jit(solution)/shard_map/ppermute | solution.py:21
  108.5 23.7 %collective-permute-start.11 = (bf16[1152,256]{1,0:T(8,128)(2,1)S(1)}, bf16[1152,256]{1,0:T(8,128)(2,1)S(1)}, u32[]{:S(2)}, u32[]{:S(2)}) collective-permute-start(bf16[1152,256]{1,0:T(8,128)(2,1)S(1)} %pad_maximum_fusion.3), channel_id=1, source_target_pairs={{0,3},{1,0},{2,1},{3,2},{4,7},{5,4},{6,5},{7,6},{8,11},{9,8},{10,9... | collective-permute-start | bytes 1769480 | tf_op jit(solution)/shard_map/ppermute | solution.py:21
  113.6 18.6 %collective-permute-start.12 = (bf16[1152,256]{1,0:T(8,128)(2,1)S(1)}, bf16[1152,256]{1,0:T(8,128)(2,1)S(1)}, u32[]{:S(2)}, u32[]{:S(2)}) collective-permute-start(bf16[1152,256]{1,0:T(8,128)(2,1)S(1)} %pad_maximum_fusion.4), channel_id=1, source_target_pairs={{0,2},{1,3},{2,0},{3,1},{4,6},{5,7},{6,4},{7,5},{8,10},{9,11},{10,... | collective-permute-start | bytes 1769480 | tf_op jit(solution)/shard_map/ppermute | solution.py:21
  115.2 29.3 %collective-permute-start.13 = (bf16[1152,256]{1,0:T(8,128)(2,1)S(1)}, bf16[1152,256]{1,0:T(8,128)(2,1)S(1)}, u32[]{:S(2)}, u32[]{:S(2)}) collective-permute-start(bf16[1152,256]{1,0:T(8,128)(2,1)S(1)} %pad_maximum_fusion.5), channel_id=1, source_target_pairs={{0,1},{1,2},{2,3},{3,0},{4,5},{5,6},{6,7},{7,4},{8,9},{9,10},{10,1... | collective-permute-start | bytes 1769480 | tf_op jit(solution)/shard_map/ppermute | solution.py:21
  146.0 9.1 %collective-permute-start.16 = (bf16[640,256]{1,0:T(8,128)(2,1)}, bf16[640,256]{1,0:T(8,128)(2,1)}, u32[]{:S(2)}, u32[]{:S(2)}) collective-permute-start(bf16[640,256]{1,0:T(8,128)(2,1)} %bitcast.55), channel_id=1, source_target_pairs={{0,3},{1,0},{2,1},{3,2},{4,7},{5,4},{6,5},{7,6},{8,11},{9,8},{10,9... | collective-permute-start | bytes 983048 | tf_op jit(solution)/shard_map/ppermute | solution.py:21
  147.1 8.8 %collective-permute-start.14 = (bf16[640,256]{1,0:T(8,128)(2,1)}, bf16[640,256]{1,0:T(8,128)(2,1)S(1)}, u32[]{:S(2)}, u32[]{:S(2)}) collective-permute-start(bf16[640,256]{1,0:T(8,128)(2,1)} %bitcast.51), channel_id=1, source_target_pairs={{0,1},{1,2},{2,3},{3,0},{4,5},{5,6},{6,7},{7,4},{8,9},{9,10},{10,1... | collective-permute-start | bytes 983048 | tf_op jit(solution)/shard_map/ppermute | solution.py:21
  149.0 12.3 %collective-permute-start.15 = (bf16[640,256]{1,0:T(8,128)(2,1)}, bf16[640,256]{1,0:T(8,128)(2,1)S(1)}, u32[]{:S(2)}, u32[]{:S(2)}) collective-permute-start(bf16[640,256]{1,0:T(8,128)(2,1)} %bitcast.53), channel_id=1, source_target_pairs={{0,2},{1,3},{2,0},{3,1},{4,6},{5,7},{6,4},{7,5},{8,10},{9,11},{10,... | collective-permute-start | bytes 983048 | tf_op jit(solution)/shard_map/ppermute | solution.py:21
  168.8 41.1 %collective-permute-start.17 = (bf16[4,40,1792]{2,1,0:T(8,128)(2,1)}, bf16[4,40,1792]{2,1,0:T(8,128)(2,1)}, u32[]{:S(2)}, u32[]{:S(2)}) collective-permute-start(bf16[4,40,1792]{2,1,0:T(8,128)(2,1)} %bitcast.58), channel_id=1, source_target_pairs={{0,12},{1,13},{2,14},{3,15},{4,0},{5,1},{6,2},{7,3},{8,4},{9,5},{1... | collective-permute-start | bytes 1720328 | tf_op jit(solution)/shard_map/ppermute | solution.py:21
  181.6 28.3 %collective-permute-start.18 = (bf16[4,40,1792]{2,1,0:T(8,128)(2,1)}, bf16[4,40,1792]{2,1,0:T(8,128)(2,1)}, u32[]{:S(2)}, u32[]{:S(2)}) collective-permute-start(bf16[4,40,1792]{2,1,0:T(8,128)(2,1)} %bitcast.59), channel_id=1, source_target_pairs={{0,4},{1,5},{2,6},{3,7},{4,8},{5,9},{6,10},{7,11},{8,12},{9,13},{1... | collective-permute-start | bytes 1720328 | tf_op jit(solution)/shard_map/ppermute | solution.py:21
  181.6 28.3 %collective-permute-start.19 = (bf16[4,40,1792]{2,1,0:T(8,128)(2,1)S(1)}, bf16[4,40,1792]{2,1,0:T(8,128)(2,1)}, u32[]{:S(2)}, u32[]{:S(2)}) collective-permute-start(bf16[4,40,1792]{2,1,0:T(8,128)(2,1)S(1)} %bitcast.226), channel_id=1, source_target_pairs={{0,8},{1,9},{2,10},{3,11},{4,12},{5,13},{6,14},{7,15},{8,0},{9,1},... | collective-permute-start | bytes 1720328 | tf_op jit(solution)/shard_map/ppermute | solution.py:21
  183.3 18.6 %collective-permute-start.23 = (bf16[512,256]{1,0:T(8,128)(2,1)S(1)}, bf16[512,256]{1,0:T(8,128)(2,1)S(1)}, u32[]{:S(2)}, u32[]{:S(2)}) collective-permute-start(bf16[512,256]{1,0:T(8,128)(2,1)S(1)} %bitcast.242), channel_id=1, source_target_pairs={{0,3},{1,0},{2,1},{3,2},{4,7},{5,4},{6,5},{7,6},{8,11},{9,8},{10,9... | collective-permute-start | bytes 786440 | tf_op jit(solution)/shard_map/ppermute | solution.py:21
  186.5 6.9 %collective-permute-start.21 = (bf16[512,256]{1,0:T(8,128)(2,1)S(1)}, bf16[512,256]{1,0:T(8,128)(2,1)S(1)}, u32[]{:S(2)}, u32[]{:S(2)}) collective-permute-start(bf16[512,256]{1,0:T(8,128)(2,1)S(1)} %bitcast.244), channel_id=1, source_target_pairs={{0,1},{1,2},{2,3},{3,0},{4,5},{5,6},{6,7},{7,4},{8,9},{9,10},{10,1... | collective-permute-start | bytes 786440 | tf_op jit(solution)/shard_map/ppermute | solution.py:21
  193.4 6.7 %collective-permute-start.22 = (bf16[512,256]{1,0:T(8,128)(2,1)S(1)}, bf16[512,256]{1,0:T(8,128)(2,1)S(1)}, u32[]{:S(2)}, u32[]{:S(2)}) collective-permute-start(bf16[512,256]{1,0:T(8,128)(2,1)S(1)} %bitcast.243), channel_id=1, source_target_pairs={{0,2},{1,3},{2,0},{3,1},{4,6},{5,7},{6,4},{7,5},{8,10},{9,11},{10,... | collective-permute-start | bytes 786440 | tf_op jit(solution)/shard_map/ppermute | solution.py:21
  205.5 23.8 %all-to-all-start.2 = ((bf16[4,4,32,1792]{3,2,1,0:T(8,128)(2,1)}), bf16[4,4,32,1792]{3,2,1,0:T(8,128)(2,1)}, u32[]{:S(2)}, u32[]{:S(2)}) async-start(bf16[4,4,32,1792]{3,2,1,0:T(8,128)(2,1)} %pad_maximum_fusion.2), calls=%async_computation.2 | async-start | bytes 3670016 | tf_op jit(solution)/shard_map/all_to_all | solution.py:69
  212.6 25.7 %collective-permute-start.26 = (bf16[80,1792]{1,0:T(8,128)(2,1)}, bf16[80,1792]{1,0:T(8,128)(2,1)S(1)}, u32[]{:S(2)}, u32[]{:S(2)}) collective-permute-start(bf16[80,1792]{1,0:T(8,128)(2,1)} %pad_maximum_fusion.19), channel_id=1, source_target_pairs={{0,17},{1,18},{2,19},{3,16},{4,21},{5,22},{6,23},{7,20},{8,25},{9,... | collective-permute-start | bytes 860168 | tf_op jit(solution)/shard_map/ppermute | solution.py:33
  218.8 19.6 %collective-permute-start.25 = (bf16[80,1792]{1,0:T(8,128)(2,1)}, bf16[80,1792]{1,0:T(8,128)(2,1)S(1)}, u32[]{:S(2)}, u32[]{:S(2)}) collective-permute-start(bf16[80,1792]{1,0:T(8,128)(2,1)} %pad_maximum_fusion.18), channel_id=1, source_target_pairs={{0,18},{1,19},{2,16},{3,17},{4,22},{5,23},{6,20},{7,21},{8,26},{9,... | collective-permute-start | bytes 860168 | tf_op jit(solution)/shard_map/ppermute | solution.py:33
  219.8 21.3 %collective-permute-start.24 = (bf16[80,1792]{1,0:T(8,128)(2,1)}, bf16[80,1792]{1,0:T(8,128)(2,1)}, u32[]{:S(2)}, u32[]{:S(2)}) collective-permute-start(bf16[80,1792]{1,0:T(8,128)(2,1)} %pad_maximum_fusion.17), channel_id=1, source_target_pairs={{0,19},{1,16},{2,17},{3,18},{4,23},{5,20},{6,21},{7,22},{8,27},{9,... | collective-permute-start | bytes 860168 | tf_op jit(solution)/shard_map/ppermute | solution.py:33
  224.2 17.4 %collective-permute-start.20 = (bf16[80,1792]{1,0:T(8,128)(2,1)}, bf16[80,1792]{1,0:T(8,128)(2,1)}, u32[]{:S(2)}, u32[]{:S(2)}) collective-permute-start(bf16[80,1792]{1,0:T(8,128)(2,1)} %pad_maximum_fusion.16), channel_id=1, source_target_pairs={{0,16},{1,17},{2,18},{3,19},{4,20},{5,21},{6,22},{7,23},{8,24},{9,... | collective-permute-start | bytes 860168 | tf_op jit(solution)/shard_map/ppermute | solution.py:33
  231.5 13.2 %collective-permute-start.27 = (bf16[64,1792]{1,0:T(8,128)(2,1)S(1)}, bf16[64,1792]{1,0:T(8,128)(2,1)S(1)}, u32[]{:S(2)}, u32[]{:S(2)}) collective-permute-start(bf16[64,1792]{1,0:T(8,128)(2,1)S(1)} %pad_maximum_fusion.26), channel_id=1, source_target_pairs={{0,16},{1,17},{2,18},{3,19},{4,20},{5,21},{6,22},{7,23},{8,24},{9,... | collective-permute-start | bytes 688136 | tf_op jit(solution)/shard_map/ppermute | solution.py:33
  238.3 10.7 %collective-permute-start.28 = (bf16[64,1792]{1,0:T(8,128)(2,1)S(1)}, bf16[64,1792]{1,0:T(8,128)(2,1)S(1)}, u32[]{:S(2)}, u32[]{:S(2)}) collective-permute-start(bf16[64,1792]{1,0:T(8,128)(2,1)S(1)} %pad_maximum_fusion.27), channel_id=1, source_target_pairs={{0,19},{1,16},{2,17},{3,18},{4,23},{5,20},{6,21},{7,22},{8,27},{9,... | collective-permute-start | bytes 688136 | tf_op jit(solution)/shard_map/ppermute | solution.py:33
  238.4 12.3 %collective-permute-start.29 = (bf16[64,1792]{1,0:T(8,128)(2,1)S(1)}, bf16[64,1792]{1,0:T(8,128)(2,1)S(1)}, u32[]{:S(2)}, u32[]{:S(2)}) collective-permute-start(bf16[64,1792]{1,0:T(8,128)(2,1)S(1)} %pad_maximum_fusion.28), channel_id=1, source_target_pairs={{0,18},{1,19},{2,16},{3,17},{4,22},{5,23},{6,20},{7,21},{8,26},{9,... | collective-permute-start | bytes 688136 | tf_op jit(solution)/shard_map/ppermute | solution.py:33
  241.0 11.8 %collective-permute-start.30 = (bf16[64,1792]{1,0:T(8,128)(2,1)S(1)}, bf16[64,1792]{1,0:T(8,128)(2,1)S(1)}, u32[]{:S(2)}, u32[]{:S(2)}) collective-permute-start(bf16[64,1792]{1,0:T(8,128)(2,1)S(1)} %pad_maximum_fusion.29), channel_id=1, source_target_pairs={{0,17},{1,18},{2,19},{3,16},{4,21},{5,22},{6,23},{7,20},{8,25},{9,... | collective-permute-start | bytes 688136 | tf_op jit(solution)/shard_map/ppermute | solution.py:33
